TPU v7x, 256 devices: a whole 4x4x8 slice. The times are simulated.
256 devices in a mesh: expert: 16 (over z, core), edata: 4 (over x), tensor: 4 (over y).
Axes of the slice: x: 4, y: 4, z: 8, core: 2. Of those that a mesh axis runs over, the one named last changes fastest.
Arguments:
- out_grad: bfloat16 [4096, 3072], P(('expert', 'edata')), may hold values from -6 to 6
- router_probs: bfloat16 [4096, 4], P(('expert', 'edata')), may hold values from 0.049804688 to 0.5
- expert_ids: int32 [4096, 4], P(('expert', 'edata')), may hold values from 0 to 15, all different within a row; in each aligned block of 64 rows (0 to 63, 64 to 127, ...) at most 24 rows name the same one
- saved_gate: bfloat16 [16, 4, 16, 24, 5632], P('expert', 'edata', None, None, 'tensor'), may hold values from -6 to 6
- saved_up: bfloat16 [16, 4, 16, 24, 5632], P('expert', 'edata', None, None, 'tensor'), may hold values from -28 to 28
- down_weight: bfloat16 [16, 3072, 5632], P('expert', 'edata', 'tensor'), may hold values from -0.078125 to 0.078125
Outputs:
- gate_grad: bfloat16 [16, 4, 16, 24, 5632], P('expert', 'edata', None, None, 'tensor')
- up_grad: bfloat16 [16, 4, 16, 24, 5632], P('expert', 'edata', None, None, 'tensor')
- weight_grad: bfloat16 [16, 3072, 5632], P('expert', 'edata', 'tensor')
- router_grad: float32 [4096, 4], P(('expert', 'edata'))
Inputs may be any that keep to these rules, and one draw needn't show every extreme that they name: `expert_ids`: each token names 4 different experts; among the 64 tokens of one shard no expert is named more than 24 times, and in some shards one is named exactly 24 times.
All inputs are finite; a program needn't handle non-finite values. Where the computation divides by a largest or mean magnitude, that divisor is 1e-20 or more.
Results may differ from a plain program's by a relative error of at most 0.012.
Values may be sent and summed in bfloat16 or wider, within the bound.
A program may use at most 128 MiB of HBM per device.

v0:
```python
import jax
import jax.numpy as jnp
from jax import lax
from jax.sharding import PartitionSpec as P


def silu_backward(d_hidden, gate_value, up_value):
    sigmoid_gate = jax.nn.sigmoid(gate_value)
    activated = gate_value * sigmoid_gate
    gate_delta = d_hidden * up_value * sigmoid_gate * (1.0 + gate_value * (1.0 - sigmoid_gate))
    up_delta = d_hidden * activated
    return (activated * up_value, gate_delta, up_delta)


def shards(out_grad, router_probs, expert_ids, saved_gate, saved_up, down_weight):
    token_count, choose_count = expert_ids.shape
    expert_count = lax.axis_size("expert")
    capacity = saved_gate.shape[3]
    model_width = out_grad.shape[1]
    local_hidden = saved_gate.shape[4]
    flat_ids = expert_ids.reshape(-1)
    matches = (flat_ids[:, None] == jnp.arange(expert_count, dtype=jnp.int32)[None, :]).astype(
        jnp.int32
    )
    earlier = jnp.cumsum(matches, axis=0) - matches
    slot_index = jnp.sum(earlier * matches, axis=1)
    target = flat_ids * capacity + slot_index
    send_probs = (
        jnp.zeros((expert_count * capacity,), jnp.bfloat16).at[target].set(router_probs.reshape(-1))
    )
    send_probs = send_probs.reshape(expert_count, capacity)
    send_rows = (
        jnp.zeros((expert_count * capacity, model_width), jnp.bfloat16)
        .at[target]
        .set(jnp.repeat(out_grad, choose_count, axis=0))
    )
    send_rows = send_rows.reshape(expert_count, capacity, model_width)
    arrived_rows, arrived_probs = (
        lax.all_to_all(send_rows, "expert", split_axis=0, concat_axis=0, tiled=True),
        lax.all_to_all(send_probs, "expert", split_axis=0, concat_axis=0, tiled=True),
    )
    slot_count = arrived_rows.shape[0] * capacity
    routed = arrived_rows.reshape(slot_count, model_width)
    routed_probs = arrived_probs.reshape(slot_count, 1).astype(jnp.float32)
    back_grad = jnp.dot(
        routed,
        lax.all_gather(down_weight, "edata", axis=1, tiled=True)[0],
        preferred_element_type=jnp.float32,
    )
    gate_value = saved_gate.reshape(slot_count, local_hidden).astype(jnp.float32)
    up_value = saved_up.reshape(slot_count, local_hidden).astype(jnp.float32)
    hidden, gate_delta, up_delta = silu_backward(routed_probs * back_grad, gate_value, up_value)
    router_part = jnp.sum(hidden * back_grad, axis=1).reshape(-1, capacity)
    local_peaks = (jnp.max(jnp.abs(gate_delta)), jnp.max(jnp.abs(up_delta)))
    gate_peak, up_peak = lax.pmax((local_peaks[0], local_peaks[1]), ("edata", "tensor"))
    gate_grad = (gate_delta / (gate_peak + 1e-06)).astype(jnp.bfloat16).reshape(saved_gate.shape)
    up_grad = (up_delta / (up_peak + 1e-06)).astype(jnp.bfloat16).reshape(saved_up.shape)
    router_total = lax.psum(router_part, "tensor")
    returned = lax.all_to_all(router_total, "expert", split_axis=0, concat_axis=0, tiled=True)
    router_grad = returned.reshape(-1)[target].reshape(token_count, choose_count)
    scaled_rows = (routed.astype(jnp.float32) * routed_probs).astype(jnp.bfloat16)
    hidden_rounded = hidden.astype(jnp.bfloat16)
    own_slice = lax.all_to_all(scaled_rows, "edata", split_axis=1, concat_axis=0, tiled=True)
    all_hidden = lax.all_gather(hidden_rounded, "edata", axis=0, tiled=True)
    weight_sum = lax.dot_general(
        own_slice, all_hidden, (((0,), (0,)), ((), ())), preferred_element_type=jnp.float32
    )
    weight_grad = weight_sum.astype(jnp.bfloat16).reshape(down_weight.shape)
    return (gate_grad, up_grad, weight_grad, router_grad)


def solution(mesh):
    in_specs = (
        P(("expert", "edata"), None),
        P(("expert", "edata"), None),
        P(("expert", "edata"), None),
        P("expert", "edata", None, None, "tensor"),
        P("expert", "edata", None, None, "tensor"),
        P("expert", "edata", "tensor"),
    )
    out_specs = (
        P("expert", "edata", None, None, "tensor"),
        P("expert", "edata", None, None, "tensor"),
        P("expert", "edata", "tensor"),
        P(("expert", "edata"), None),
    )
    return jax.shard_map(shards, mesh=mesh, in_specs=in_specs, out_specs=out_specs, check_vma=False)
```

profile of v0, /device:TPU:2, one launch (start us, length us, event | category | flops | bytes accessed | tf_op | source)
XLA Modules:
  0.0 239.5 jit_solution(12054494272669398714)
XLA Ops:
  7.2 0.0 copy-start.3
  7.2 0.0 all-gather.3.cloned.1.call-start
  7.2 0.7 all-gather.3.cloned.1.call-update
  7.9 0.0 copy-done.3
  7.9 0.1 copy.24
  8.0 0.1 eq.29
  8.1 0.1 eq.25
  8.3 0.6 reduce-window.6
  8.9 0.2 slice_reduce_fusion
  9.1 0.1 copy.23
  9.2 0.1 mul.62
  9.3 0.1 copy.27
  9.4 0.1 reshape.147
  9.5 0.1 fusion.14
  9.6 2.2 scatter_custom_fusion
  11.8 0.7 all_to_all.35
  12.5 8.6 %all-to-all-start = ((bf16[16,1,24]{2,1,0:T(2,128)(2,1)}), bf16[16,1,24]{2,1,0:T(2,128)(2,1)S(1)}, u32[]{:S(2)}, u32[]{:S(2)}) async-start(bf16[16,1,24]{2,1,0:T(2,128)(2,1)} %all_to_all.35), calls=%async_computation | async-start | bytes 16384 | tf_op jit(solution)/shard_map/all_to_all | solution.py:40
  21.1 0.5 broadcast_in_dim.15
  21.6 0.4 reshape.155
  22.0 4.5 %scatter_custom_fusion.1 = bf16[384,3072]{1,0:T(8,128)(2,1)} fusion(s32[256]{0:T(256)S(1)} %bitcast.63, bf16[256,3072]{1,0:T(8,128)(2,1)S(1)} %reshape.155, bf16[]{:T(256)} %constant.8.clone.1), kind=kCustom, calls=%fused_computation.26 | custom fusion | bytes 2359298 | tf_op jit(solution)/shard_map/scatter | solution.py:35
  26.5 2.1 all-to-all-done
  28.6 5.3 %all-to-all-start.1 = ((bf16[16,24,3072]{2,1,0:T(8,128)(2,1)}), bf16[16,24,3072]{2,1,0:T(8,128)(2,1)S(1)}, u32[]{:S(2)}, u32[]{:S(2)}) async-start(bf16[16,24,3072]{2,1,0:T(8,128)(2,1)} %bitcast.58), calls=%async_computation.1 | async-start | bytes 4718592 | tf_op jit(solution)/shard_map/all_to_all | solution.py:39
  33.9 0.0 all-gather.5.cloned.1.call-start
  33.9 0.1 reshape.131
  34.0 54.8 %all-to-all-done.1 = bf16[16,24,3072]{2,1,0:T(8,128)(2,1)S(1)} async-done(((bf16[16,24,3072]{2,1,0:T(8,128)(2,1)}), bf16[16,24,3072]{2,1,0:T(8,128)(2,1)S(1)}, u32[]{:S(2)}, u32[]{:S(2)}) %all-to-all-start.1) | async-done | bytes 2359328 | tf_op jit(solution)/shard_map/all_to_all | solution.py:39
  88.8 11.9 %all-gather.3.cloned.1.call-done = bf16[1,3072,1408]{2,1,0:T(8,128)(2,1)} async-done(((bf16[1,768,1408]{2,1,0:T(8,128)(2,1)}), bf16[1,3072,1408]{2,1,0:T(8,128)(2,1)}) %all-gather.3.cloned.1.call-update) | async-done | bytes 8650768 | tf_op jit(solution)/shard_map/all_gather | solution.py:47
  100.7 10.5 %multiply_reduce_fusion = (f32[384]{0:T(512)S(1)}, f32[]{:T(128)}, f32[]{:T(128)}, f32[384,1408]{1,0:T(8,128)}, bf16[384,1408]{1,0:T(8,128)(2,1)}, /*index=5*/f32[384,1408]{1,0:T(8,128)}) fusion(bf16[1,1,16,24,1408]{4,3,2,1,0:T(8,128)(2,1)} %param.10, bf16[1,1,16,24,1408]{4,3,2,1,0:T(8,128)(2,1)S(1)} %copy-done.1, f32[384]{0:T(512)S(1)} %reshape.131, ...), kind=kOutput, calls=%fused_computation.19 | convolution fusion | flops 3333783040 | bytes 18582536 | tf_op jit(solution)/shard_map/dot_general | solution.py:45
  111.2 0.0 all-gather.5.cloned.1.call-update
  111.2 3.8 %reshape.134 = f32[384,4,768]{2,1,0:T(4,128)} reshape(bf16[16,24,3072]{2,1,0:T(8,128)(2,1)S(1)} %all-to-all-done.1) | data formatting | bytes 7077888 | tf_op jit(solution)/shard_map/convert_element_type | solution.py:61
  114.9 0.1 all_to_all.33
  115.0 11.2 %psum.7 = f32[16,1,24]{2,1,0:T(1,128)} all-reduce(f32[16,1,24]{2,1,0:T(1,128)S(1)} %all_to_all.33), channel_id=1, replica_groups=mesh['expert'=16,'edata'=4,'tensor'=4] {'tensor'}, use_global_device_ids=true, to_apply=%region_10.11 | all-reduce | flops 384 | bytes 3072 | tf_op jit(solution)/shard_map/psum | solution.py:58
  126.2 7.1 %all-to-all-start.3 = ((f32[16,1,24]{2,1,0:T(1,128)}), f32[16,1,24]{2,1,0:T(1,128)S(1)}, u32[]{:S(2)}, u32[]{:S(2)}) async-start(f32[16,1,24]{2,1,0:T(1,128)} %psum.7), calls=%async_computation.3 | async-start | bytes 16384 | tf_op jit(solution)/shard_map/all_to_all | solution.py:59
  133.3 3.3 %multiply_convert_fusion = bf16[384,4,768]{2,1,0:T(4,128)(2,1)S(1)} fusion(f32[384,4,768]{2,1,0:T(4,128)} %reshape.134, f32[384]{0:T(512)S(1)} %reshape.131), kind=kLoop, calls=%fused_computation.5 | loop fusion | flops 2359296 | bytes 7079424 | tf_op jit(solution)/shard_map/convert_element_type | solution.py:61
  136.6 1.7 copy.29
  138.3 2.5 %all-to-all-done.3 = f32[16,1,24]{2,1,0:T(1,128)S(1)} async-done(((f32[16,1,24]{2,1,0:T(1,128)}), f32[16,1,24]{2,1,0:T(1,128)S(1)}, u32[]{:S(2)}, u32[]{:S(2)}) %all-to-all-start.3) | async-done | bytes 1568 | tf_op jit(solution)/shard_map/all_to_all | solution.py:59
  140.8 4.5 %all-to-all-start.2 = ((bf16[384,4,768]{2,0,1:T(8,128)(2,1)}), bf16[384,4,768]{2,0,1:T(8,128)(2,1)S(1)}, u32[]{:S(2)}, u32[]{:S(2)}) async-start(bf16[384,4,768]{2,0,1:T(8,128)(2,1)} %copy.29), calls=%async_computation.2 | async-start | bytes 4718592 | tf_op jit(solution)/shard_map/all_to_all | solution.py:63
  145.3 70.0 %all-reduce = (f32[]{:T(128)}, f32[]{:T(128)}) all-reduce(f32[]{:T(128)} %get-tuple-element.22, f32[]{:T(128)} %get-tuple-element.17), channel_id=1, replica_groups=mesh['expert'=16,'edata'=4,'tensor'=4] {'edata','tensor'}, use_global_device_ids=true, to_apply=%region_6.7 | all-reduce | flops 2 | bytes 16 | tf_op jit(solution)/shard_map/pmax | solution.py:55
  216.7 2.9 %divide_convert_fusion.1 = bf16[384,1408]{1,0:T(8,128)(2,1)} fusion(f32[384,1408]{1,0:T(8,128)} %get-tuple-element.23, f32[]{:T(128)S(6)} %add.40), kind=kLoop, calls=%fused_computation.22 | loop fusion | flops 1081344 | bytes 3244036 | tf_op jit(solution)/shard_map/convert_element_type | solution.py:56
  219.5 0.0 copy-done
  219.6 1.9 divide_convert_fusion
  221.4 0.5 broadcast.80
  221.9 0.7 reduce.9
  222.6 0.1 reshape.128
  222.7 1.9 gather_fusion
  224.6 0.1 reshape.129
  224.7 0.7 copy.30
  225.4 0.0 all-to-all-done.2
  225.4 7.3 %fusion.2 = bf16[1,768,1408]{2,1,0:T(8,128)(2,1)} fusion(bf16[1536,768]{1,0:T(8,128)(2,1)S(1)} %bitcast.59, bf16[1536,1408]{1,0:T(8,128)(2,1)} %all-gather.5.cloned.1.call-done), kind=kOutput, calls=%fused_computation.10 | convolution fusion | flops 3322970112 | bytes 8847360 | tf_op jit(solution)/shard_map/dot_general | solution.py:65
  (15 shorter events, 0.1 us)
Async XLA Ops:
  7.2 0.8 copy-start.3
  7.2 2.1 copy-start.4
  7.2 13.9 %copy-start.2 = (bf16[64,3072]{1,0:T(8,128)(2,1)S(1)}, bf16[64,3072]{1,0:T(8,128)(2,1)}, u32[]{:S(2)}) copy-start(bf16[64,3072]{1,0:T(8,128)(2,1)} %param.6) | copy-start | bytes 1179652
  7.2 93.5 %all-gather.3.cloned.1.call-start = ((), (), s32[]{:S(2)}) async-start(), calls=%async_computation.4 | async-start | bytes 10813440 | tf_op jit(solution)/shard_map/all_gather | solution.py:47
  12.5 16.1 %all-to-all-start = ((bf16[16,1,24]{2,1,0:T(2,128)(2,1)}), bf16[16,1,24]{2,1,0:T(2,128)(2,1)S(1)}, u32[]{:S(2)}, u32[]{:S(2)}) async-start(bf16[16,1,24]{2,1,0:T(2,128)(2,1)} %all_to_all.35), calls=%async_computation | async-start | bytes 16384 | tf_op jit(solution)/shard_map/all_to_all | solution.py:40
  28.6 72.1 %copy-start.1 = (bf16[1,1,16,24,1408]{4,3,2,1,0:T(8,128)(2,1)S(1)}, bf16[1,1,16,24,1408]{4,3,2,1,0:T(8,128)(2,1)}, u32[]{:S(2)}) copy-start(bf16[1,1,16,24,1408]{4,3,2,1,0:T(8,128)(2,1)} %param.9) | copy-start | bytes 3244036
  28.6 60.2 %all-to-all-start.1 = ((bf16[16,24,3072]{2,1,0:T(8,128)(2,1)}), bf16[16,24,3072]{2,1,0:T(8,128)(2,1)S(1)}, u32[]{:S(2)}, u32[]{:S(2)}) async-start(bf16[16,24,3072]{2,1,0:T(8,128)(2,1)} %bitcast.58), calls=%async_computation.1 | async-start | bytes 4718592 | tf_op jit(solution)/shard_map/all_to_all | solution.py:39
  33.9 191.6 %all-gather.5.cloned.1.call-start = ((), (), s32[]{:S(2)}) async-start(), calls=%async_computation.5 | async-start | bytes 5406720 | tf_op jit(solution)/shard_map/all_gather | solution.py:64
  126.2 14.6 %all-to-all-start.3 = ((f32[16,1,24]{2,1,0:T(1,128)}), f32[16,1,24]{2,1,0:T(1,128)S(1)}, u32[]{:S(2)}, u32[]{:S(2)}) async-start(f32[16,1,24]{2,1,0:T(1,128)} %psum.7), calls=%async_computation.3 | async-start | bytes 16384 | tf_op jit(solution)/shard_map/all_to_all | solution.py:59
  140.8 84.6 %all-to-all-start.2 = ((bf16[384,4,768]{2,0,1:T(8,128)(2,1)}), bf16[384,4,768]{2,0,1:T(8,128)(2,1)S(1)}, u32[]{:S(2)}, u32[]{:S(2)}) async-start(bf16[384,4,768]{2,0,1:T(8,128)(2,1)} %copy.29), calls=%async_computation.2 | async-start | bytes 4718592 | tf_op jit(solution)/shard_map/all_to_all | solution.py:63
  216.7 2.9 %copy-start = (f32[384,1408]{1,0:T(8,128)S(1)}, f32[384,1408]{1,0:T(8,128)}, u32[]{:S(2)}) copy-start(f32[384,1408]{1,0:T(8,128)} %get-tuple-element.25) | copy-start | bytes 6488068
Sparse Core Ops, SparseCore 0:
  9.8 90.8 all-gather.2
  111.3 74.7 all-gather.4
where the time goes:
time: 240 us
  blocking collectives  81.2 us (34%)
  waiting for transfers between devices  72 us (30%)
  starting transfers between devices  25.5 us (11%)
  local copies, waits for them, and re-layouts  18.2 us (8%)
  matrix products  17.7 us (7%)
  between operations  15.5 us (6%)
  other arithmetic  9.45 us (4%)
    pmax x1, blocking collectives, shards(): lax.pmax((local_peaks[0], local_peaks[1]), ('edata', 'tensor'))  70 us
    all_to_all x1, waiting for transfers between devices, shards(): lax.all_to_all(send_rows, 'expert', split_axis=0, concat_axis=0, tiled=True)  54.8 us
    all_gather x1, waiting for transfers between devices, shards(): lax.all_gather(down_weight, 'edata', axis=1, tiled=True)[0]  11.9 us
    psum x1, blocking collectives, shards(): router_total = lax.psum(router_part, 'tensor')  11.2 us
    dot_general x1, matrix products, shards(): jnp.dot(routed, lax.all_gather(down_weight, 'edata', axis=1, tiled=True)[...  10.5 us
    all_to_all x1, starting transfers between devices, shards(): lax.all_to_all(send_probs, 'expert', split_axis=0, concat_axis=0, tiled=T...  8.57 us
    dot_general x1, matrix products, shards(): lax.dot_general(own_slice, all_hidden, (((0,), (0,)), ((), ())), preferre...  7.27 us
    all_to_all x1, starting transfers between devices, shards(): lax.all_to_all(router_total, 'expert', split_axis=0, concat_axis=0, tiled...  7.12 us
  transfers between devices with their start and end apart: 6, of which 4 were waited for; matrix products, arithmetic and copies ran while one was open for 11% of the time, Pallas kernels for 0%

commit v1 on v0

v1 whole, which is shorter than its diff:
```python
import functools

import jax
import jax.numpy as jnp
from jax import lax
from jax.experimental import pallas as pl
from jax.experimental.pallas import tpu as pltpu
from jax.sharding import PartitionSpec as P

MESH = pl.DeviceIdType.MESH
RING = 4
F32 = jnp.float32
BF16 = jnp.bfloat16


def local(src, dst, sem):
    return pltpu.make_async_copy(src, dst, sem)


def silu_factors(gate_value, up_value):
    sigmoid_gate = jax.nn.sigmoid(gate_value)
    activated = gate_value * sigmoid_gate
    gate_factor = up_value * sigmoid_gate * (1.0 + gate_value * (1.0 - sigmoid_gate))
    return activated * up_value, gate_factor, activated


def kernel(
    experts, cap, tok, top,
    og, ids_ref, probs_ref, gate, up, w,
    gate_out, up_out, wg_out, router_out,
    gate_v, up_v, w_v, a_gate, a_up, hid, rows, x2, meta_own, meta_in, target_v, scale_v, sb,
    sb_o, sb_d, sb_c, rb_o, rb_d, rb_c, keep, own, wg_v, g_v, u_v,
    pk_own, pk_in, rl, rz_out, rz_in, ry_own, ry_in,
    load_sem, xs, xr, ms, mr, zs, zr, ys, yr_, hs, hr, bs, br, ps, pr, ws, wr, vs, vr, out_sem,
):
    e, x, y = lax.axis_index("expert"), lax.axis_index("edata"), lax.axis_index("tensor")
    z, c = lax.div(e, 2), lax.rem(e, 2)
    slots, width = gate.shape
    half = slots // 2
    quarter = half // 2
    features = w.shape[0]
    lanes_half = features // 2
    pair = 2 * cap
    x_right, x_left, x_far = lax.rem(x + 1, RING), lax.rem(x + 3, RING), lax.rem(x + 2, RING)
    y_right, y_left, y_far = lax.rem(y + 1, RING), lax.rem(y + 3, RING), lax.rem(y + 2, RING)
    first, second = pl.ds(0, half), pl.ds(half, half)

    loads = []
    for i, part in enumerate((first, second)):
        loads.append((
            local(gate.at[part], gate_v.at[part], load_sem.at[2 * i]),
            local(up.at[part], up_v.at[part], load_sem.at[2 * i + 1]),
        ))
    load_w = local(w, w_v, load_sem.at[4])
    for pair_of in loads:
        for copy in pair_of:
            copy.start()
    load_w.start()

    barrier = pltpu.get_barrier_semaphore()

    def greet(device):
        pl.semaphore_signal(barrier, inc=1, device_id=device, device_id_type=MESH)

    @pl.loop(1, experts)
    def _(i):
        greet((lax.rem(e + i, experts), x, y))

    @pl.loop(1, RING * RING)
    def _(i):
        p = lax.rem(x * RING + y + i, RING * RING)
        greet((e, lax.div(p, RING), lax.rem(p, RING)))

    @pl.when(x != y)
    def _():
        greet((2 * z + 1 - c, y, x))

    place = (
        lax.broadcasted_iota(jnp.int32, (tok, 128), 1)
        == lax.broadcasted_iota(jnp.int32, (tok, 128), 0) + tok * c
    ).astype(F32).astype(BF16)
    meta_own[0:top, :] = jnp.dot(
        ids_ref[...].astype(F32).astype(BF16), place, preferred_element_type=F32
    )
    meta_own[4:4 + top, :] = jnp.dot(probs_ref[...], place, preferred_element_type=F32)

    peers = experts - 1 + RING * RING - 1
    pl.semaphore_wait(barrier, jnp.where(x == y, peers, peers + 1))

    def swap(core):
        lanes = pl.ds(pl.multiple_of(features * y + lanes_half * core, 128), lanes_half)
        device = (2 * z + core, y, x)
        return (
            pltpu.make_async_remote_copy(
                src_ref=meta_own, dst_ref=meta_in.at[c], send_sem=ms.at[core],
                recv_sem=mr.at[c], device_id=device, device_id_type=MESH,
            ),
            pltpu.make_async_remote_copy(
                src_ref=og.at[:, lanes], dst_ref=x2.at[c], send_sem=xs.at[core],
                recv_sem=xr.at[c], device_id=device, device_id_type=MESH,
            ),
        )

    for core in range(2):
        at_home = jnp.logical_and(x == y, c == core)

        @pl.when(at_home)
        def _():
            lanes = pl.ds(pl.multiple_of(features * y + lanes_half * core, 128), lanes_half)
            local(meta_own, meta_in.at[c], mr.at[c]).start()
            local(og.at[:, lanes], x2.at[c], xr.at[c]).start()

        @pl.when(jnp.logical_not(at_home))
        def _():
            for copy in swap(core):
                copy.start()

    def ring_copy(buf, block, part, axis, to_right, send, recv, index):
        if axis == "edata":
            device = (e, x_right if to_right else x_left, y)
        else:
            device = (e, x, y_right if to_right else y_left)
        return pltpu.make_async_remote_copy(
            src_ref=buf.at[block, part], dst_ref=buf.at[block, part],
            send_sem=send.at[index], recv_sem=recv.at[index],
            device_id=device, device_id_type=MESH,
        )

    def ring(buf, me, left, right, axis, send, recv):
        make = functools.partial(ring_copy, buf, axis=axis, send=send, recv=recv)
        return dict(
            r0=make(block=me, part=first, to_right=True, index=0),
            r1=make(block=me, part=second, to_right=True, index=1),
            l0=make(block=me, part=first, to_right=False, index=2),
            l1=make(block=me, part=second, to_right=False, index=3),
            rf=make(block=left, part=first, to_right=True, index=4),
            lf=make(block=right, part=second, to_right=False, index=5),
        )

    h_ring = ring(hid, x, x_left, x_right, "edata", hs, hr)
    y_ring = ring(rows, y, y_left, y_right, "tensor", ys, yr_)

    def hidden_of(base):
        @pl.loop(0, half // 16)
        def _(i):
            part = pl.ds(pl.multiple_of(base + i * 16, 16), 16)
            hidden, gate_factor, up_factor = silu_factors(
                gate_v[part, :].astype(F32), up_v[part, :].astype(F32)
            )
            hid[x, part, :] = hidden.astype(BF16)
            a_gate[part, :] = gate_factor
            a_up[part, :] = up_factor

    for copy in loads[0]:
        copy.wait()
    hidden_of(0)
    h_ring["r0"].start()
    for copy in loads[1]:
        copy.wait()
    hidden_of(half)
    h_ring["l1"].start()
    h_ring["r1"].start()
    h_ring["l0"].start()

    for core in range(2):
        local(meta_own, meta_in.at[core], mr.at[core]).wait()
        local(x2.at[core], x2.at[core], xr.at[core]).wait()
    meta = meta_in[0] + meta_in[1]
    lane = lax.broadcasted_iota(jnp.int32, (experts, 128), 1)
    expert_row = lax.broadcasted_iota(jnp.int32, (experts, 128), 0).astype(F32)
    member = jnp.zeros((experts, 128), F32)
    scale = jnp.zeros((experts, 128), F32)
    for k in range(top):
        named = meta[k:k + 1, :] == expert_row
        member = jnp.where(named, 1.0, member)
        scale = jnp.where(named, meta[4 + k:5 + k, :], scale)
    live = lane < 2 * tok
    member = jnp.where(live, member, 0.0)
    row_i = lax.broadcasted_iota(jnp.int32, (128, 128), 0)
    lane_i = lax.broadcasted_iota(jnp.int32, (128, 128), 1)
    before = jnp.logical_and(row_i < lane_i, jnp.logical_or(row_i >= tok, lane_i < tok))
    earlier = jnp.dot(
        member.astype(BF16), before.astype(F32).astype(BF16), preferred_element_type=F32
    )
    target_v[...] = jnp.where(
        member > 0.0, earlier + jnp.where(lane >= tok, float(cap), 0.0), -1.0
    )
    scale_v[...] = scale
    slot_row = lax.broadcasted_iota(jnp.int32, (pair, 128), 0).astype(F32)
    my_rows = pl.ds(pl.multiple_of(pair * z, 16), pair)
    my_lanes = pl.ds(pl.multiple_of(lanes_half * c, 128), lanes_half)

    def dispatch(to):
        return pltpu.make_async_remote_copy(
            src_ref=sb.at[pl.ds(pl.multiple_of(pair * to, 16), pair)],
            dst_ref=rows.at[y, my_rows, my_lanes],
            send_sem=zs.at[to], recv_sem=zr.at[e],
            device_id=(to, x, y), device_id_type=MESH,
        )

    @pl.loop(0, experts)
    def _(i):
        to = lax.rem(e + i + 1, experts)
        pick = jnp.where(
            slot_row == target_v[pl.ds(to, 1), :], scale_v[pl.ds(to, 1), :], 0.0
        ).astype(BF16)
        tokens = x2[...].reshape(2 * tok, lanes_half)
        block = jnp.dot(pick[:, :2 * tok], tokens, preferred_element_type=F32)
        sb[pl.ds(pl.multiple_of(pair * to, 16), pair), :] = block.astype(BF16)

        @pl.when(to != e)
        def _():
            dispatch(to).start()

        @pl.when(to == e)
        def _():
            local(
                sb.at[pl.ds(pl.multiple_of(pair * to, 16), pair)],
                rows.at[y, my_rows, my_lanes], zr.at[e],
            ).start()

    def arrived(start):
        @pl.loop(start, start + experts // 2)
        def _(s):
            at = rows.at[
                y, pl.ds(pl.multiple_of(pair * lax.div(s, 2), 16), pair),
                pl.ds(pl.multiple_of(lanes_half * lax.rem(s, 2), 128), lanes_half),
            ]
            local(at, at, zr.at[s]).wait()

    arrived(0)
    y_ring["r0"].start()
    y_ring["l0"].start()
    arrived(experts // 2)
    y_ring["l1"].start()
    y_ring["r1"].start()

    h_ring["r0"].wait_recv()
    h_ring["rf"].start()
    h_ring["l1"].wait_recv()
    h_ring["lf"].start()
    y_ring["r0"].wait_recv()
    y_ring["rf"].start()
    y_ring["l1"].wait_recv()
    y_ring["lf"].start()
    load_w.wait()
    for name in ("r1", "l0", "rf", "lf"):
        y_ring[name].wait_recv()

    tiles = [(at, min(256, width - at)) for at in range(0, width, 256)]

    def partial(replica, store0, store1):
        block = rows[replica]
        for at, size in tiles:
            product = jnp.dot(block, w_v[:, at:at + size], preferred_element_type=F32)
            store0(at, size, product[:half])
            store1(at, size, product[half:])

    def keep_in(ref, kind):
        def store(at, size, value):
            ref[:, at:at + size] = value.astype(kind)
        return store

    def send(index, src, dst, to_right):
        return pltpu.make_async_remote_copy(
            src_ref=src, dst_ref=dst, send_sem=bs.at[index], recv_sem=br.at[index],
            device_id=(e, x_right if to_right else x_left, y), device_id_type=MESH,
        )

    part_a, part_b = pl.ds(0, quarter), pl.ds(quarter, quarter)
    far0 = send(0, sb_o.at[0], rb_o.at[0], True)
    far1 = send(1, sb_o.at[1], rb_o.at[1], False)
    near0 = send(2, sb_d.at[0], rb_d.at[0], True)
    near1 = send(3, sb_d.at[1], rb_d.at[1], False)
    both = [
        (send(4 + 2 * i, sb_c.at[0, part], rb_c.at[0, part], True),
         send(5 + 2 * i, sb_c.at[1, part], rb_c.at[1, part], False))
        for i, part in enumerate((part_a, part_b))
    ]
    partial(x_far, keep_in(sb_o.at[0], BF16), keep_in(sb_o.at[1], BF16))
    far0.start()
    far1.start()
    partial(x_right, keep_in(keep.at[0], F32), keep_in(sb_d.at[0], BF16))
    near0.start()
    partial(x_left, keep_in(sb_d.at[1], BF16), keep_in(keep.at[1], F32))
    near1.start()
    partial(x, keep_in(own.at[0], F32), keep_in(own.at[1], F32))

    for name in ("r1", "l0", "rf", "lf"):
        h_ring[name].wait_recv()
    all_hidden = hid[...].reshape(RING * slots, width)
    step = 256 if features % 256 == 0 else 128
    wg_copies = []
    for i in range(features // step):
        at = pl.ds(i * step, step)
        wg_v[at, :] = lax.dot_general(
            rows[:, :, i * step:(i + 1) * step].reshape(RING * slots, step), all_hidden,
            (((0,), (0,)), ((), ())), preferred_element_type=F32,
        ).astype(BF16)
        wg_copies.append(local(wg_v.at[at], wg_out.at[at], out_sem.at[i]))
        wg_copies[-1].start()

    far0.wait_recv()
    far1.wait_recv()
    for i, pair_of in enumerate(both):
        @pl.loop(0, quarter // 16)
        def _(j):
            part = pl.ds(pl.multiple_of(i * quarter + j * 16, 16), 16)
            for side in range(2):
                sb_c[side, part, :] = (
                    keep[side, part, :] + rb_o[side, part, :].astype(F32)
                ).astype(BF16)
        for copy in pair_of:
            copy.start()
    near0.wait_recv()
    near1.wait_recv()

    zero = jnp.zeros((16, 128), F32)
    peaks = (zero, zero)
    for i, pair_of in enumerate(both):
        for copy in pair_of:
            copy.wait_recv()
        for side in range(2):
            def body(j, carry):
                gate_peak, up_peak = carry
                part = pl.ds(pl.multiple_of(i * quarter + j * 16, 16), 16)
                at = pl.ds(pl.multiple_of(side * half + i * quarter + j * 16, 16), 16)
                sent = rb_d[1 - side, part, :].astype(F32) + rb_c[side, part, :].astype(F32)
                d_hidden = own[side, part, :] + sent
                gate_delta = d_hidden * a_gate[at, :]
                up_delta = d_hidden * a_up[at, :]
                a_gate[at, :] = gate_delta
                a_up[at, :] = up_delta
                weighted = up_delta * up_v[at, :].astype(F32)
                total = zero
                for lane0 in range(0, width, 128):
                    sl = slice(lane0, lane0 + 128)
                    gate_peak = jnp.maximum(gate_peak, jnp.abs(gate_delta[:, sl]))
                    up_peak = jnp.maximum(up_peak, jnp.abs(up_delta[:, sl]))
                    total = total + weighted[:, sl]
                rl[at, :] = total
                return gate_peak, up_peak

            peaks = lax.fori_loop(0, quarter // 16, body, peaks)
    for i in range(2):
        pk_own[i] = jnp.maximum(peaks[i][:8], peaks[i][8:])
    me = x * RING + y
    pk_in[me] = pk_own[...]

    def tell_peak(p):
        return pltpu.make_async_remote_copy(
            src_ref=pk_own, dst_ref=pk_in.at[me], send_sem=ps.at[p], recv_sem=pr.at[me],
            device_id=(e, lax.div(p, RING), lax.rem(p, RING)), device_id_type=MESH,
        )

    @pl.loop(1, RING * RING)
    def _(i):
        tell_peak(lax.rem(me + i, RING * RING)).start()

    rl[slots:, :] = jnp.zeros((rl.shape[0] - slots, 128), F32)
    ones = jnp.ones((8, 128), BF16)
    across = (((1,), (1,)), ((), ()))

    def give_back(to):
        return pltpu.make_async_remote_copy(
            src_ref=rz_out.at[to], dst_ref=rz_in.at[e], send_sem=ws.at[to], recv_sem=wr.at[e],
            device_id=(to, x, y), device_id_type=MESH,
        )

    @pl.loop(0, experts)
    def _(i):
        to = lax.rem(e + i, experts)
        seg = rl[pl.ds(pl.multiple_of(cap * to, 8), 128), :]
        high = seg.astype(BF16)
        low = (seg - high.astype(F32)).astype(BF16)
        rz_out[to] = lax.dot_general(
            ones, high, across, preferred_element_type=F32
        ) + lax.dot_general(ones, low, across, preferred_element_type=F32)

        @pl.when(to != e)
        def _():
            give_back(to).start()

    rz_in[e] = rz_out[e]

    @pl.loop(1, RING * RING)
    def _(i):
        p = lax.rem(me + i, RING * RING)
        local(pk_in.at[p], pk_in.at[p], pr.at[p]).wait()

    all_peaks = jnp.max(pk_in[...], axis=0)
    gate_scale = 1.0 / (jnp.max(all_peaks[0], axis=(0, 1), keepdims=True) + 1e-6)
    up_scale = 1.0 / (jnp.max(all_peaks[1], axis=(0, 1), keepdims=True) + 1e-6)

    def scaled(base):
        @pl.loop(0, half // 16)
        def _(j):
            part = pl.ds(pl.multiple_of(base + j * 16, 16), 16)
            g_v[part, :] = (a_gate[part, :] * gate_scale).astype(BF16)
            u_v[part, :] = (a_up[part, :] * up_scale).astype(BF16)

    outs = []
    for i, part in enumerate((first, second)):
        scaled(i * half)
        outs.append(local(g_v.at[part], gate_out.at[part], out_sem.at[8 + 2 * i]))
        outs.append(local(u_v.at[part], up_out.at[part], out_sem.at[9 + 2 * i]))
        outs[-1].start()
        outs[-2].start()

    @pl.loop(1, experts)
    def _(i):
        s = lax.rem(e + i, experts)
        local(rz_in.at[s], rz_in.at[s], wr.at[s]).wait()

    ry_own[...] = rz_in[:, 0, :]

    def tell_sum(p):
        return pltpu.make_async_remote_copy(
            src_ref=ry_own, dst_ref=ry_in.at[y], send_sem=vs.at[p], recv_sem=vr.at[y],
            device_id=(e, x, p), device_id_type=MESH,
        )

    for p in (y_right, y_left, y_far):
        tell_sum(p).start()
    ids_f = ids_ref[...].astype(F32)
    expert_col = lax.broadcasted_iota(jnp.int32, (experts, tok), 0).astype(F32)
    named = [(ids_f[k:k + 1, :] == expert_col).astype(F32) for k in range(top)]
    tri = (
        lax.broadcasted_iota(jnp.int32, (tok, tok), 0)
        < lax.broadcasted_iota(jnp.int32, (tok, tok), 1)
    ).astype(F32).astype(BF16)
    earlier = jnp.dot(sum(named).astype(BF16), tri, preferred_element_type=F32)
    slot_col = lax.broadcasted_iota(jnp.int32, (128, tok), 0).astype(F32)
    at_slot = [
        slot_col == jnp.sum(earlier * named[k], axis=0, keepdims=True) for k in range(top)
    ]
    for p in (y_right, y_left, y_far):
        local(ry_in.at[p], ry_in.at[p], vr.at[p]).wait()
    sums = ry_own[...]
    for p in (y_right, y_left, y_far):
        sums = sums + ry_in[p]
    high = sums.astype(BF16)
    low = (sums - high.astype(F32)).astype(BF16)
    down = (((0,), (0,)), ((), ()))
    for k in range(top):
        pick = named[k].astype(BF16)
        found = lax.dot_general(
            high, pick, down, preferred_element_type=F32
        ) + lax.dot_general(low, pick, down, preferred_element_type=F32)
        value = jnp.sum(jnp.where(at_slot[k], found, 0.0), axis=0, keepdims=True)
        router_out[k:k + 1, :] = value / probs_ref[k:k + 1, :].astype(F32)

    for copy in wg_copies + outs:
        copy.wait()
    for core in range(2):
        @pl.when(jnp.logical_not(jnp.logical_and(x == y, c == core)))
        def _():
            for copy in swap(core):
                copy.wait_send()

    @pl.loop(1, experts)
    def _(i):
        to = lax.rem(e + i, experts)
        dispatch(to).wait_send()
        give_back(to).wait_send()

    @pl.loop(1, RING * RING)
    def _(i):
        tell_peak(lax.rem(me + i, RING * RING)).wait_send()

    for p in (y_right, y_left, y_far):
        tell_sum(p).wait_send()
    for name in ("r0", "r1", "l0", "l1", "rf", "lf"):
        h_ring[name].wait_send()
        y_ring[name].wait_send()
    for copy in (far0, far1, near0, near1) + both[0] + both[1]:
        copy.wait_send()


def shards(out_grad, router_probs, expert_ids, saved_gate, saved_up, down_weight):
    tok, top = expert_ids.shape
    experts = lax.axis_size("expert")
    cap = saved_gate.shape[3]
    width = saved_gate.shape[4]
    slots = saved_gate.shape[2] * cap
    features = down_weight.shape[1]
    half = slots // 2
    any_space = pl.BlockSpec(memory_space=pl.ANY)
    vmem = pl.BlockSpec(memory_space=pltpu.VMEM)
    dma = pltpu.SemaphoreType.DMA
    gate_grad, up_grad, weight_grad, router_grad = pl.pallas_call(
        functools.partial(kernel, experts, cap, tok, top),
        out_shape=(
            jax.ShapeDtypeStruct((slots, width), BF16),
            jax.ShapeDtypeStruct((slots, width), BF16),
            jax.ShapeDtypeStruct((features, width), BF16),
            jax.ShapeDtypeStruct((top, tok), F32),
        ),
        in_specs=[any_space, vmem, vmem, any_space, any_space, any_space],
        out_specs=(any_space, any_space, any_space, vmem),
        scratch_shapes=[
            pltpu.VMEM((slots, width), BF16),
            pltpu.VMEM((slots, width), BF16),
            pltpu.VMEM((features, width), BF16),
            pltpu.VMEM((slots, width), F32),
            pltpu.VMEM((slots, width), F32),
            pltpu.VMEM((RING, slots, width), BF16),
            pltpu.VMEM((RING, slots, features), BF16),
            pltpu.VMEM((2, tok, features // 2), BF16),
            pltpu.VMEM((8, 128), F32),
            pltpu.VMEM((2, 8, 128), F32),
            pltpu.VMEM((experts, 128), F32),
            pltpu.VMEM((experts, 128), F32),
            pltpu.VMEM((2 * cap * experts, features // 2), BF16),
            pltpu.VMEM((2, half, width), BF16),
            pltpu.VMEM((2, half, width), BF16),
            pltpu.VMEM((2, half, width), BF16),
            pltpu.VMEM((2, half, width), BF16),
            pltpu.VMEM((2, half, width), BF16),
            pltpu.VMEM((2, half, width), BF16),
            pltpu.VMEM((2, half, width), F32),
            pltpu.VMEM((2, half, width), F32),
            pltpu.VMEM((features, width), BF16),
            pltpu.VMEM((slots, width), BF16),
            pltpu.VMEM((slots, width), BF16),
            pltpu.VMEM((2, 8, 128), F32),
            pltpu.VMEM((RING * RING, 2, 8, 128), F32),
            pltpu.VMEM((slots + 128, 128), F32),
            pltpu.VMEM((experts, 8, 128), F32),
            pltpu.VMEM((experts, 8, 128), F32),
            pltpu.VMEM((experts, 128), F32),
            pltpu.VMEM((RING, experts, 128), F32),
            dma((5,)),
            dma((2,)), dma((2,)), dma((2,)), dma((2,)),
            dma((experts,)), dma((experts,)),
            dma((6,)), dma((6,)), dma((6,)), dma((6,)),
            dma((8,)), dma((8,)),
            dma((RING * RING,)), dma((RING * RING,)),
            dma((experts,)), dma((experts,)),
            dma((RING,)), dma((RING,)),
            dma((12,)),
        ],
        compiler_params=pltpu.CompilerParams(
            collective_id=0, has_side_effects=True, vmem_limit_bytes=56 * 1024 * 1024
        ),
        cost_estimate=pl.CostEstimate(
            flops=4 * RING * slots * features * width,
            bytes_accessed=8 * slots * width + 4 * features * width,
            transcendentals=slots * width,
        ),
    )(
        out_grad, expert_ids.T, router_probs.T, saved_gate.reshape(slots, width),
        saved_up.reshape(slots, width), down_weight.reshape(features, width),
    )
    return (
        gate_grad.reshape(saved_gate.shape), up_grad.reshape(saved_up.shape),
        weight_grad.reshape(down_weight.shape), router_grad.T,
    )


def solution(mesh):
    in_specs = (
        P(("expert", "edata"), None),
        P(("expert", "edata"), None),
        P(("expert", "edata"), None),
        P("expert", "edata", None, None, "tensor"),
        P("expert", "edata", None, None, "tensor"),
        P("expert", "edata", "tensor"),
    )
    out_specs = (
        P("expert", "edata", None, None, "tensor"),
        P("expert", "edata", None, None, "tensor"),
        P("expert", "edata", "tensor"),
        P(("expert", "edata"), None),
    )
    return jax.shard_map(shards, mesh=mesh, in_specs=in_specs, out_specs=out_specs, check_vma=False)
```

time: 240 us -> 115 us (0.48)
  the two profiles are of different devices: /device:TPU:2 before, /device:TPU:1 now
where the time goes in v1:
time: 115 us
  Pallas kernels  108 us (94%)
  local copies, waits for them, and re-layouts  6.31 us (5%)
    pallas_call x1, Pallas kernels, shards(): pl.pallas_call(functools.partial(kernel, experts, cap, tok, top), out_sha...  108 us
    unnamed x10, local copies, waits for them, and re-layouts  6.31 us

profile of v1, /device:TPU:1, one launch (start us, length us, event | category | flops | bytes accessed | tf_op | source)
XLA Modules:
  0.0 115.3 jit_solution(1364463976830484494)
XLA Ops:
  0.6 108.3 %shard_map.93 = (bf16[384,1408]{1,0:T(8,128)(2,1)}, bf16[384,1408]{1,0:T(8,128)(2,1)}, bf16[768,1408]{1,0:T(8,128)(2,1)}, f32[4,64]{1,0:T(4,128)}) custom-call(bf16[64,3072]{1,0:T(8,128)(2,1)} %og.1, s32[4,64]{1,0:T(4,128)} %bitcast.16, bf16[4,64]{1,0:T(4,128)(2,1)} %bitcast.17, bf16[384,1408]{1,0:T(8,128)(2,1)} %bitcast.14, bf16[384,1408]{1,0:T(8,128)(2,1)} %bitcast.15, ...), custom_call_target="tpu_custom_call" | custom-call | flops 6643777536 | bytes 8650752 | tf_op jit(solution)/shard_map/pallas_call | solution.py:491
  108.9 0.0 copy-start.1
  108.9 2.4 %copy.14 = bf16[1,1,16,24,1408]{4,3,2,1,0:T(8,128)(2,1)} copy(bf16[1,1,16,24,1408]{4,3,2,1,0:T(8,128)(2,1)} %bitcast.11) | data formatting | bytes 2162688
  111.3 0.0 copy-done.1
  111.3 0.0 copy-start
  111.3 1.0 copy.15
  112.3 1.0 copy-done
  113.3 0.0 copy-start.2
  113.3 1.3 %copy.16 = bf16[1,768,1408]{2,1,0:T(8,128)(2,1)} copy(bf16[1,768,1408]{2,1,0:T(8,128)(2,1)S(1)} %bitcast.9) | data formatting | bytes 4325376
  114.7 0.0 copy-done.2
  114.7 0.6 copy.17
Async XLA Ops:
  108.9 2.4 %copy-start.1 = (bf16[384,1408]{1,0:T(8,128)(2,1)S(1)}, bf16[384,1408]{1,0:T(8,128)(2,1)}, u32[]{:S(2)}) copy-start(bf16[384,1408]{1,0:T(8,128)(2,1)} %get-tuple-element.9) | copy-start | bytes 3244036
  111.3 2.0 %copy-start = (bf16[768,1408]{1,0:T(8,128)(2,1)S(1)}, bf16[768,1408]{1,0:T(8,128)(2,1)}, u32[]{:S(2)}) copy-start(bf16[768,1408]{1,0:T(8,128)(2,1)} %get-tuple-element.10) | copy-start | bytes 6488068
  113.3 1.3 %copy-start.2 = (f32[4,64]{1,0:T(4,128)S(1)}, f32[4,64]{1,0:T(4,128)}, u32[]{:S(2)}) copy-start(f32[4,64]{1,0:T(4,128)} %get-tuple-element.11) | copy-start | bytes 3076

commit v2 on v1

v2 whole, which is shorter than its diff:
```python
import functools

import jax
import jax.numpy as jnp
from jax import lax
from jax.experimental import pallas as pl
from jax.experimental.pallas import tpu as pltpu
from jax.sharding import PartitionSpec as P

MESH = pl.DeviceIdType.MESH
RING = 4
F32 = jnp.float32
BF16 = jnp.bfloat16


def local(src, dst, sem):
    return pltpu.make_async_copy(src, dst, sem)


def silu_factors(gate_value, up_value):
    sigmoid_gate = jax.nn.sigmoid(gate_value)
    activated = gate_value * sigmoid_gate
    gate_factor = up_value * sigmoid_gate * (1.0 + gate_value * (1.0 - sigmoid_gate))
    return activated * up_value, gate_factor, activated


def kernel(
    experts, cap, tok, top,
    og, ids, probs, gate, up, w,
    gate_out, up_out, wg_out, router_out,
    ids_ref, probs_ref, og_v, gate_v, up_v, w_v, a_gate, a_up, hid, rows, x2, meta_own, meta_in, sb,
    part_f, part_b, sb_c, rb_o, rb_d, rb_c, wg_acc,
    pk_own, pk_in, pk_row, pk_rows, rl, rz_out, rz_in, ry_own, ry_in,
    load_sem, xs, xr, ms, mr, zs, zr, ys, yr, hs, hr, bs, br, ps, pr, qs, qr, ws, wr, vs, vr,
):
    e, x, y = lax.axis_index("expert"), lax.axis_index("edata"), lax.axis_index("tensor")
    z, c = lax.div(e, 2), lax.rem(e, 2)
    slots, width = gate.shape
    half = slots // 2
    quarter = half // 2
    features = w.shape[0]
    lanes_half = features // 2
    pair = 2 * cap
    x_right, x_left, x_far = lax.rem(x + 1, RING), lax.rem(x + 3, RING), lax.rem(x + 2, RING)
    y_right, y_left, y_far = lax.rem(y + 1, RING), lax.rem(y + 3, RING), lax.rem(y + 2, RING)
    first, second = pl.ds(0, half), pl.ds(half, half)

    def share(core):
        return lax.rem(y - x + 2 * core + RING, RING)

    from_y = lax.rem(x + y + 2 * c, RING)
    gives_home = jnp.logical_and(share(1 - c) == x, x == y)
    takes_home = jnp.logical_and(from_y == y, x == y)
    stays = jnp.logical_and(share(c) == x, x == y)

    loads = []
    for i, part in enumerate((first, second)):
        loads.append((
            local(gate.at[part], gate_v.at[part], load_sem.at[2 * i]),
            local(up.at[part], up_v.at[part], load_sem.at[2 * i + 1]),
        ))
    load_w = local(w, w_v, load_sem.at[4])
    small = (
        local(ids, ids_ref, load_sem.at[5]),
        local(probs, probs_ref, load_sem.at[6]),
    ) + tuple(
        local(
            og.at[:, pl.ds(
                pl.multiple_of(features * share(core) + lanes_half * core, 128), lanes_half
            )],
            og_v.at[core], load_sem.at[7 + core],
        )
        for core in range(2)
    )
    for copy in small:
        copy.start()
    for pair_of in loads:
        for copy in pair_of:
            copy.start()
    load_w.start()

    barrier = pltpu.get_barrier_semaphore()

    def greet(device):
        pl.semaphore_signal(barrier, inc=1, device_id=device, device_id_type=MESH)

    @pl.loop(1, experts)
    def _(i):
        greet((lax.rem(e + i, experts), x, y))

    @pl.loop(1, RING * RING)
    def _(i):
        p = lax.rem(x * RING + y + i, RING * RING)
        greet((e, lax.div(p, RING), lax.rem(p, RING)))

    @pl.when(jnp.logical_not(gives_home))
    def _():
        greet((2 * z + 1 - c, share(1 - c), x))

    @pl.when(jnp.logical_not(takes_home))
    def _():
        greet((2 * z + 1 - c, y, from_y))

    place = (
        lax.broadcasted_iota(jnp.int32, (tok, 128), 1)
        == lax.broadcasted_iota(jnp.int32, (tok, 128), 0) + tok * c
    ).astype(F32).astype(BF16)
    for copy in small:
        copy.wait()
    meta_own[0:top, :] = jnp.dot(
        ids_ref[...].astype(F32).astype(BF16), place, preferred_element_type=F32
    )
    meta_own[4:4 + top, :] = jnp.dot(probs_ref[...], place, preferred_element_type=F32)

    for i in range(2):
        for copy in loads[i]:
            copy.wait()

        @pl.loop(0, half // 32)
        def _(j):
            part = pl.ds(pl.multiple_of(i * half + j * 32, 32), 32)
            for at in range(0, width, 128):
                lanes = slice(at, at + 128)
                hidden, gate_factor, up_factor = silu_factors(
                    gate_v[part, lanes].astype(F32), up_v[part, lanes].astype(F32)
                )
                hid[x, part, lanes] = hidden.astype(BF16)
                a_gate[part, lanes] = gate_factor
                a_up[part, lanes] = up_factor

    peers = experts - 1 + RING * RING - 1
    pl.semaphore_wait(barrier, peers + jnp.where(gives_home, 0, 1) + jnp.where(takes_home, 0, 1))

    def swap(core):
        device = (2 * z + core, share(core), x)
        return (
            pltpu.make_async_remote_copy(
                src_ref=meta_own, dst_ref=meta_in.at[c], send_sem=ms.at[core],
                recv_sem=mr.at[c], device_id=device, device_id_type=MESH,
            ),
            pltpu.make_async_remote_copy(
                src_ref=og_v.at[core], dst_ref=x2.at[c], send_sem=xs.at[core],
                recv_sem=xr.at[c], device_id=device, device_id_type=MESH,
            ),
        )

    for core in range(2):
        at_home = jnp.logical_and(stays, c == core)

        @pl.when(at_home)
        def _():
            local(meta_own, meta_in.at[c], mr.at[c]).start()
            local(og_v.at[core], x2.at[c], xr.at[c]).start()

        @pl.when(jnp.logical_not(at_home))
        def _():
            for copy in swap(core):
                copy.start()

    part_a, part_e = pl.ds(0, quarter), pl.ds(quarter, quarter)
    eighth = quarter // 2
    part_c, part_d = pl.ds(quarter, eighth), pl.ds(quarter + eighth, eighth)
    far_a = pl.ds(half, quarter)
    far_c, far_d = (pl.ds(half + quarter + i * eighth, eighth) for i in range(2))

    def pass_hidden(index, block, part, to_right):
        at = hid.at[block, part]
        return pltpu.make_async_remote_copy(
            src_ref=at, dst_ref=at, send_sem=hs.at[index], recv_sem=hr.at[index],
            device_id=(e, x_right if to_right else x_left, y), device_id_type=MESH,
        )

    h_r0 = pass_hidden(0, x, first, True)
    h_r1 = pass_hidden(1, x, second, True)
    h_l0 = pass_hidden(2, x, first, False)
    h_l1 = pass_hidden(3, x, second, False)
    h_ra = pass_hidden(4, x_left, part_a, True)
    h_la = pass_hidden(5, x_right, far_a, False)
    h_rc = pass_hidden(6, x_left, part_c, True)
    h_lc = pass_hidden(7, x_right, far_c, False)
    h_rd = pass_hidden(8, x_left, part_d, True)
    h_ld = pass_hidden(9, x_right, far_d, False)
    for copy in (h_r0, h_l1, h_r1, h_l0):
        copy.start()
    for core in range(2):
        local(meta_own, meta_in.at[core], mr.at[core]).wait()
        local(x2.at[core], x2.at[core], xr.at[core]).wait()
    meta = meta_in[0] + meta_in[1]
    lane = lax.broadcasted_iota(jnp.int32, (experts, 128), 1)
    expert_row = lax.broadcasted_iota(jnp.int32, (experts, 128), 0).astype(F32)
    member = jnp.zeros((experts, 128), F32)
    scale = jnp.zeros((experts, 128), F32)
    for k in range(top):
        named = meta[k:k + 1, :] == expert_row
        member = jnp.where(named, 1.0, member)
        scale = jnp.where(named, meta[4 + k:5 + k, :], scale)
    live = lane < 2 * tok
    member = jnp.where(live, member, 0.0)
    row_i = lax.broadcasted_iota(jnp.int32, (128, 128), 0)
    lane_i = lax.broadcasted_iota(jnp.int32, (128, 128), 1)
    before = jnp.logical_and(row_i < lane_i, jnp.logical_or(row_i >= tok, lane_i < tok))
    earlier = jnp.dot(
        member.astype(BF16), before.astype(F32).astype(BF16), preferred_element_type=F32
    )
    target = jnp.where(
        member > 0.0, earlier + jnp.where(lane >= tok, float(cap), 0.0), -1.0
    )
    slot_row = lax.broadcasted_iota(jnp.int32, (experts, pair, 128), 1).astype(F32)
    pick = jnp.where(slot_row == target[:, None, :], scale[:, None, :], 0.0).astype(BF16)
    sb[...] = jnp.dot(
        pick.reshape(experts * pair, 128)[:, :2 * tok], x2[...].reshape(2 * tok, lanes_half),
        preferred_element_type=F32,
    ).astype(BF16)
    my_rows = pl.ds(pl.multiple_of(pair * z, 16), pair)
    my_lanes = pl.ds(pl.multiple_of(lanes_half * c, 128), lanes_half)

    def dispatch(to):
        return pltpu.make_async_remote_copy(
            src_ref=sb.at[pl.ds(pl.multiple_of(pair * to, 16), pair)],
            dst_ref=rows.at[y, my_rows, my_lanes],
            send_sem=zs.at[to], recv_sem=zr.at[e],
            device_id=(to, x, y), device_id_type=MESH,
        )

    chips = experts // 2

    def chip(j):
        away = lax.div(j + 1, 2)
        return lax.rem(jnp.where(lax.rem(j, 2) == 1, z + away, z - away + chips), chips)

    local(
        sb.at[pl.ds(pl.multiple_of(pair * e, 16), pair)], rows.at[y, my_rows, my_lanes], zr.at[e]
    ).start()
    dispatch(2 * z + 1 - c).start()

    def dispatch_both(j):
        for core in range(2):
            dispatch(2 * chip(j) + core).start()

    @pl.loop(1, chips)
    def _(j):
        dispatch_both(j)

    def pass_rows(j, block, to_right, index):
        at = rows.at[block, pl.ds(pl.multiple_of(pair * chip(j), 16), pair)]
        return pltpu.make_async_remote_copy(
            src_ref=at, dst_ref=at, send_sem=ys.at[index], recv_sem=yr.at[index],
            device_id=(e, x, y_right if to_right else y_left), device_id_type=MESH,
        )

    def go_right(j):
        return pass_rows(j, y, True, j)

    def go_left(j):
        return pass_rows(j, y, False, chips + j)

    def on_right(j):
        return pass_rows(j, y_left, True, 2 * chips + j)

    def on_left(j):
        return pass_rows(j, y_right, False, 2 * chips + j)

    def start_own(j):
        for core in range(2):
            at = rows.at[
                y, pl.ds(pl.multiple_of(pair * chip(j), 16), pair),
                pl.ds(lanes_half * core, lanes_half),
            ]
            local(at, at, zr.at[2 * chip(j) + core]).wait()
        go_right(j).start()
        go_left(j).start()

    def start_on(j):
        go_right(j).wait_recv()
        go_left(j).wait_recv()

        (on_right, on_left)[j % 2](j).start()

    tiles = [(at, min(256, width - at)) for at in range(0, width, 256)]

    def send(index, src, dst, to_right):
        return pltpu.make_async_remote_copy(
            src_ref=src, dst_ref=dst, send_sem=bs.at[index], recv_sem=br.at[index],
            device_id=(e, x_right if to_right else x_left, y), device_id_type=MESH,
        )

    far0 = send(0, part_b.at[2, 0], rb_o.at[0], True)
    far1 = send(1, part_b.at[2, 1], rb_o.at[1], False)
    near0, near1 = (
        [
            send(8 + 2 * i + k, part_b.at[role, 1 - k, part], rb_d.at[k, part], k == 0)
            for i, part in enumerate((part_a, part_e))
        ]
        for k, role in enumerate((1, 3))
    )
    both = [
        (send(4 + 2 * i, sb_c.at[0, part], rb_c.at[0, part], True),
         send(5 + 2 * i, sb_c.at[1, part], rb_c.at[1, part], False))
        for i, part in enumerate((part_a, part_e))
    ]

    def partial(replica):
        role = lax.rem(replica - x + RING, RING)
        block = rows[replica]
        for at, size in tiles:
            product = jnp.dot(block, w_v[:, at:at + size], preferred_element_type=F32)
            for i in range(2):
                value = product[i * half:(i + 1) * half]
                part_f[role, i, :, at:at + size] = value
                part_b[role, i, :, at:at + size] = value.astype(BF16)

        @pl.when(role == 2)
        def _():
            far0.start()
            far1.start()

        @pl.when(role == 1)
        def _():
            near0[0].start()

        @pl.when(role == 3)
        def _():
            near1[0].start()

    for j in range(chips):
        start_own(j)

    @pl.when(x == y)
    def _():
        h_r0.wait_recv()
        h_rc.start()
        h_l1.wait_recv()
        h_lc.start()

    load_w.wait()
    partial(y)

    for k in range(chips):
        start_on(k)

    partial(jnp.where(x == y_right, y_left, y_right))
    partial(jnp.where(x == y_right, y_right, y_left))

    @pl.loop(0, chips)
    def _(j):
        @pl.when(lax.rem(j, 2) == 0)
        def _():
            on_right(j).wait_recv()

        @pl.when(lax.rem(j, 2) == 1)
        def _():
            on_left(j).wait_recv()

    partial(y_far)
    near0[1].start()
    near1[1].start()

    @pl.when(x != y)
    def _():
        h_r0.wait_recv()
        h_l1.wait_recv()

    for copy in (h_r1, h_l0):
        copy.wait_recv()
    step = 256 if features % 256 == 0 else 128

    def outer(block, slot_parts, at):
        left = jnp.concatenate([rows[block, p, at:at + step] for p in slot_parts], axis=0)
        right = jnp.concatenate([hid[block, p, :] for p in slot_parts], axis=0)
        return lax.dot_general(
            left, right, (((0,), (0,)), ((), ())), preferred_element_type=F32
        )

    everything = (slice(0, slots),)
    for at in range(0, features, step):
        wg_acc[at:at + step, :] = (
            outer(x, everything, at) + outer(x_left, everything, at) + outer(x_right, everything, at)
        )
    early = (slice(0, quarter), slice(half, half + quarter))
    late = [
        tuple(slice(at + i * eighth, at + (i + 1) * eighth) for at in (quarter, half + quarter))
        for i in range(2)
    ]

    for core in range(2):
        @pl.when(jnp.logical_not(jnp.logical_and(stays, c == core)))
        def _():
            for copy in swap(core):
                copy.wait_send()

    @pl.loop(1, experts)
    def _(i):
        dispatch(lax.rem(e + i, experts)).wait_send()

    @pl.loop(0, chips)
    def _(j):
        go_right(j).wait_send()
        go_left(j).wait_send()

        @pl.when(lax.rem(j, 2) == 0)
        def _():
            on_right(j).wait_send()

        @pl.when(lax.rem(j, 2) == 1)
        def _():
            on_left(j).wait_send()

    def pass_on(side):
        @pl.when(side == 0)
        def _():
            far0.wait_recv()

        @pl.when(side == 1)
        def _():
            far1.wait_recv()

        for i in range(2):
            @pl.loop(0, quarter // 16)
            def _(j):
                part = pl.ds(pl.multiple_of(i * quarter + j * 16, 16), 16)
                sb_c[side, part, :] = (
                    part_f[1 + 2 * side, side, part, :] + rb_o[side, part, :].astype(F32)
                ).astype(BF16)

            for k in range(2):
                @pl.when(side == k)
                def _():
                    both[i][k].start()

        @pl.when(side == 0)
        def _():
            h_ra.start()

        @pl.when(side == 1)
        def _():
            h_la.start()

        @pl.when(jnp.logical_and(side == 0, x != y))
        def _():
            h_rc.start()

        @pl.when(jnp.logical_and(side == 1, x != y))
        def _():
            h_lc.start()

    early_side = jnp.where(x_left == y, 1, 0)
    pass_on(early_side)
    pass_on(1 - early_side)
    for copy in near0 + near1:
        copy.wait_recv()

    zero = jnp.zeros((16, 128), F32)
    peaks = (zero, zero)
    for i, pair_of in enumerate(both):
        for copy in pair_of:
            copy.wait_recv()
        for side in range(2):
            def body(j, carry):
                gate_peak, up_peak = carry
                part = pl.ds(pl.multiple_of(i * quarter + j * 16, 16), 16)
                at = pl.ds(pl.multiple_of(side * half + i * quarter + j * 16, 16), 16)
                sent = rb_d[1 - side, part, :].astype(F32) + rb_c[side, part, :].astype(F32)
                d_hidden = part_f[0, side, part, :] + sent
                gate_delta = d_hidden * a_gate[at, :]
                up_delta = d_hidden * a_up[at, :]
                a_gate[at, :] = gate_delta
                a_up[at, :] = up_delta
                weighted = up_delta * up_v[at, :].astype(F32)
                total = zero
                for lane0 in range(0, width, 128):
                    sl = slice(lane0, lane0 + 128)
                    gate_peak = jnp.maximum(gate_peak, jnp.abs(gate_delta[:, sl]))
                    up_peak = jnp.maximum(up_peak, jnp.abs(up_delta[:, sl]))
                    total = total + weighted[:, sl]
                rl[at, :] = total
                return gate_peak, up_peak

            peaks = lax.fori_loop(0, quarter // 16, body, peaks)
    peak_row = lax.broadcasted_iota(jnp.int32, (8, 128), 0)
    pk_own[...] = jnp.where(
        peak_row < 4,
        jnp.max(peaks[0], axis=0, keepdims=True), jnp.max(peaks[1], axis=0, keepdims=True),
    )

    def tell_row(p):
        return pltpu.make_async_remote_copy(
            src_ref=pk_own, dst_ref=pk_in.at[y], send_sem=ps.at[p], recv_sem=pr.at[y],
            device_id=(e, x, p), device_id_type=MESH,
        )

    def tell_column(p):
        return pltpu.make_async_remote_copy(
            src_ref=pk_row, dst_ref=pk_rows.at[x], send_sem=qs.at[p], recv_sem=qr.at[x],
            device_id=(e, p, y), device_id_type=MESH,
        )

    y_others, x_others = (y_right, y_left, y_far), (x_right, x_left, x_far)
    for p in y_others:
        tell_row(p).start()

    rl[slots:, :] = jnp.zeros((rl.shape[0] - slots, 128), F32)
    ones = jnp.ones((8, 128), BF16)
    across = (((1,), (1,)), ((), ()))

    def split(value):
        high = value.astype(BF16)
        return high, (value - high.astype(F32)).astype(BF16)

    sums = sum(
        lax.dot_general(ones, part, across, preferred_element_type=F32) for part in split(rl[...])
    )
    rz_out[...] = sums[0:1, :]

    def give_back(to):
        return pltpu.make_async_remote_copy(
            src_ref=rz_out, dst_ref=rz_in.at[e], send_sem=ws.at[to], recv_sem=wr.at[e],
            device_id=(to, x, y), device_id_type=MESH,
        )

    @pl.loop(1, experts)
    def _(i):
        give_back(lax.rem(e + i, experts)).start()

    rz_in[e] = rz_out[...]
    row_peak = pk_own[...]
    for p in y_others:
        local(pk_in.at[p], pk_in.at[p], pr.at[p]).wait()
        row_peak = jnp.maximum(row_peak, pk_in[p])
    pk_row[...] = row_peak
    for p in x_others:
        tell_column(p).start()
    h_rd.start()
    h_ld.start()
    @pl.loop(1, experts)
    def _(i):
        s = lax.rem(e + i, experts)
        local(rz_in.at[s], rz_in.at[s], wr.at[s]).wait()

    from_experts = rz_in[:, 0, :]
    mine = (
        lax.broadcasted_iota(jnp.int32, (128, from_experts.shape[1]), 1)
        == lax.broadcasted_iota(jnp.int32, (128, from_experts.shape[1]), 0) + cap * e
    ).astype(F32).astype(BF16)
    ry_own[...] = sum(
        lax.dot_general(part, mine, across, preferred_element_type=F32)
        for part in split(from_experts)
    )

    def tell_sum(p):
        return pltpu.make_async_remote_copy(
            src_ref=ry_own, dst_ref=ry_in.at[y], send_sem=vs.at[p], recv_sem=vr.at[y],
            device_id=(e, x, p), device_id_type=MESH,
        )

    for p in y_others:
        tell_sum(p).start()

    for copy in (h_ra, h_la):
        copy.wait_recv()
    for at in range(0, features, step):
        wg_acc[at:at + step, :] += outer(x_far, early, at)

    all_peaks = row_peak
    for p in x_others:
        local(pk_rows.at[p], pk_rows.at[p], qr.at[p]).wait()
        all_peaks = jnp.maximum(all_peaks, pk_rows[p])
    gate_scale = 1.0 / (jnp.max(all_peaks[:4], axis=(0, 1), keepdims=True) + 1e-6)
    up_scale = 1.0 / (jnp.max(all_peaks[4:], axis=(0, 1), keepdims=True) + 1e-6)

    @pl.loop(0, slots // 16)
    def _(j):
        part = pl.ds(pl.multiple_of(j * 16, 16), 16)
        gate_out[part, :] = (a_gate[part, :] * gate_scale).astype(BF16)
        up_out[part, :] = (a_up[part, :] * up_scale).astype(BF16)

    for copy in (h_rc, h_lc):
        copy.wait_recv()
    for at in range(0, features, step):
        wg_acc[at:at + step, :] += outer(x_far, late[0], at)


    ids_f = ids_ref[...].astype(F32)
    expert_col = lax.broadcasted_iota(jnp.int32, (experts, tok), 0).astype(F32)
    named = [(ids_f[k:k + 1, :] == expert_col).astype(F32) for k in range(top)]
    tri = (
        lax.broadcasted_iota(jnp.int32, (tok, tok), 0)
        < lax.broadcasted_iota(jnp.int32, (tok, tok), 1)
    ).astype(F32).astype(BF16)
    earlier = jnp.dot(sum(named).astype(BF16), tri, preferred_element_type=F32)
    slot_col = lax.broadcasted_iota(jnp.int32, (128, tok), 0).astype(F32)
    at_slot = [
        slot_col == jnp.sum(earlier * named[k], axis=0, keepdims=True) for k in range(top)
    ]
    for p in y_others:
        local(ry_in.at[p], ry_in.at[p], vr.at[p]).wait()
    sums = ry_own[...]
    for p in y_others:
        sums = sums + ry_in[p]
    high, low = split(sums)
    down = (((0,), (0,)), ((), ()))
    for k in range(top):
        pick = named[k].astype(BF16)
        found = lax.dot_general(
            high, pick, down, preferred_element_type=F32
        ) + lax.dot_general(low, pick, down, preferred_element_type=F32)
        value = jnp.sum(jnp.where(at_slot[k], found, 0.0), axis=0, keepdims=True)
        router_out[k:k + 1, :] = value / probs_ref[k:k + 1, :].astype(F32)

    for copy in (h_rd, h_ld):
        copy.wait_recv()
    for at in range(0, features, step):
        wg_out[at:at + step, :] = (wg_acc[at:at + step, :] + outer(x_far, late[1], at)).astype(BF16)

    @pl.loop(1, experts)
    def _(i):
        to = lax.rem(e + i, experts)
        give_back(to).wait_send()

    for p in y_others:
        tell_sum(p).wait_send()
        tell_row(p).wait_send()
    for p in x_others:
        tell_column(p).wait_send()
    for copy in (h_r0, h_r1, h_l0, h_l1, h_ra, h_la, h_rc, h_lc, h_rd, h_ld):
        copy.wait_send()

    for copy in [far0, far1] + near0 + near1 + list(both[0] + both[1]):
        copy.wait_send()


def write_out(*refs):
    count = len(refs) // 2
    copies = [local(refs[i], refs[count + i], refs[-1].at[i]) for i in range(count)]
    for copy in copies:
        copy.start()
    for copy in copies:
        copy.wait()


def shards(out_grad, router_probs, expert_ids, saved_gate, saved_up, down_weight):
    tok, top = expert_ids.shape
    experts = lax.axis_size("expert")
    cap = saved_gate.shape[3]
    width = saved_gate.shape[4]
    slots = saved_gate.shape[2] * cap
    features = down_weight.shape[1]
    half = slots // 2
    chips = experts // 2
    any_space = pl.BlockSpec(memory_space=pl.ANY)
    hbm = pl.BlockSpec(memory_space=pltpu.HBM)
    vmem = pl.BlockSpec(memory_space=pltpu.VMEM)
    dma = pltpu.SemaphoreType.DMA
    stay = functools.partial(pltpu.with_memory_space_constraint, memory_space=pltpu.HBM)
    shapes = (
        ((slots, width), BF16), ((slots, width), BF16), ((features, width), BF16),
        ((top, tok), F32),
    )
    results = pl.pallas_call(
        functools.partial(kernel, experts, cap, tok, top),
        out_shape=tuple(pltpu.VMEM(*shape) for shape in shapes),
        in_specs=[hbm] * 6,
        out_specs=(vmem,) * 4,
        scratch_shapes=[
            pltpu.VMEM((top, tok), jnp.int32),
            pltpu.VMEM((top, tok), BF16),
            pltpu.VMEM((2, tok, features // 2), BF16),
            pltpu.VMEM((slots, width), BF16),
            pltpu.VMEM((slots, width), BF16),
            pltpu.VMEM((features, width), BF16),
            pltpu.VMEM((slots, width), F32),
            pltpu.VMEM((slots, width), F32),
            pltpu.VMEM((RING, slots, width), BF16),
            pltpu.VMEM((RING, slots, features), BF16),
            pltpu.VMEM((2, tok, features // 2), BF16),
            pltpu.VMEM((8, 128), F32),
            pltpu.VMEM((2, 8, 128), F32),
            pltpu.VMEM((2 * cap * experts, features // 2), BF16),
            pltpu.VMEM((RING, 2, half, width), F32),
            pltpu.VMEM((RING, 2, half, width), BF16),
            pltpu.VMEM((2, half, width), BF16),
            pltpu.VMEM((2, half, width), BF16),
            pltpu.VMEM((2, half, width), BF16),
            pltpu.VMEM((2, half, width), BF16),
            pltpu.VMEM((features, width), F32),
            pltpu.VMEM((8, 128), F32),
            pltpu.VMEM((RING, 8, 128), F32),
            pltpu.VMEM((8, 128), F32),
            pltpu.VMEM((RING, 8, 128), F32),
            pltpu.VMEM((slots + 128, 128), F32),
            pltpu.VMEM((1, slots + 128), F32),
            pltpu.VMEM((experts, 1, slots + 128), F32),
            pltpu.VMEM((experts, 128), F32),
            pltpu.VMEM((RING, experts, 128), F32),
            dma((9,)),
            dma((2,)), dma((2,)), dma((2,)), dma((2,)),
            dma((experts,)), dma((experts,)),
            dma((3 * chips,)), dma((3 * chips,)),
            dma((10,)), dma((10,)),
            dma((12,)), dma((12,)),
            dma((RING,)), dma((RING,)), dma((RING,)), dma((RING,)),
            dma((experts,)), dma((experts,)),
            dma((RING,)), dma((RING,)),
        ],
        compiler_params=pltpu.CompilerParams(
            collective_id=0, has_side_effects=True, vmem_limit_bytes=48 * 1024 * 1024
        ),
        cost_estimate=pl.CostEstimate(
            flops=4 * RING * slots * features * width,
            bytes_accessed=4 * slots * width + 2 * features * width,
            transcendentals=slots * width,
        ),
    )(
        stay(out_grad), stay(expert_ids.T), stay(router_probs.T), stay(saved_gate.reshape(slots, width)),
        stay(saved_up.reshape(slots, width)), stay(down_weight.reshape(features, width)),
    )
    gate_grad, up_grad, weight_grad, router_grad = pl.pallas_call(
        write_out,
        out_shape=tuple(jax.ShapeDtypeStruct(*shape) for shape in shapes),
        in_specs=[vmem] * 4,
        out_specs=(any_space,) * 4,
        scratch_shapes=[dma((4,))],
        compiler_params=pltpu.CompilerParams(vmem_limit_bytes=1024 * 1024),
    )(*(pltpu.with_memory_space_constraint(r, memory_space=pltpu.VMEM) for r in results))
    return (
        gate_grad.reshape(saved_gate.shape), up_grad.reshape(saved_up.shape),
        weight_grad.reshape(down_weight.shape), router_grad.T,
    )


def solution(mesh):
    in_specs = (
        P(("expert", "edata"), None),
        P(("expert", "edata"), None),
        P(("expert", "edata"), None),
        P("expert", "edata", None, None, "tensor"),
        P("expert", "edata", None, None, "tensor"),
        P("expert", "edata", "tensor"),
    )
    out_specs = (
        P("expert", "edata", None, None, "tensor"),
        P("expert", "edata", None, None, "tensor"),
        P("expert", "edata", "tensor"),
        P(("expert", "edata"), None),
    )
    return jax.shard_map(shards, mesh=mesh, in_specs=in_specs, out_specs=out_specs, check_vma=False)
```

time: 115 us -> 91 us (0.79)
  Pallas kernels: 108 us -> 90.3 us
  local copies, waits for them, and re-layouts: 6.31 us -> 0 us
    pallas_call x1, Pallas kernels: 108 us -> 88.2 us  [shards(): pl.pallas_call(functools.partial(kernel, experts, cap, tok, top), out_sha...]
    unnamed x10 -> x0, local copies, waits for them, and re-layouts: 6.31 us -> none
    pallas_call x0 -> x1, Pallas kernels: none -> 2.09 us  [shards(): pl.pallas_call(write_out, out_shape=tuple((jax.ShapeDtypeStruct(*shape) f...]
where the time goes in v2:
time: 91 us; the launch traced here: 90.9 us
  Pallas kernels  90.3 us (99%)
    pallas_call x1, Pallas kernels, shards(): pl.pallas_call(functools.partial(kernel, experts, cap, tok, top), out_sha...  88.2 us
    pallas_call x1, Pallas kernels, shards(): pl.pallas_call(write_out, out_shape=tuple((jax.ShapeDtypeStruct(*shape) f...  2.09 us

profile of v2, /device:TPU:1, one launch (start us, length us, event | category | flops | bytes accessed | tf_op | source)
XLA Modules:
  0.0 90.9 jit_solution(17365857268409775333)
XLA Ops:
  0.6 88.2 %shard_map.93 = (bf16[384,1408]{1,0:T(8,128)(2,1)S(1)}, bf16[384,1408]{1,0:T(8,128)(2,1)S(1)}, bf16[768,1408]{1,0:T(8,128)(2,1)S(1)}, f32[4,64]{1,0:T(4,128)S(1)}) custom-call(bf16[64,3072]{1,0:T(8,128)(2,1)} %og.1, s32[4,64]{1,0:T(4,128)} %bitcast.15, bf16[4,64]{1,0:T(4,128)(2,1)} %bitcast.17, bf16[384,1408]{1,0:T(8,128)(2,1)} %bitcast.11, ...), custom_call_target="tpu_custom_call" | custom-call | flops 6643777536 | bytes 4325376 | tf_op jit(solution)/shard_map/pallas_call | solution.py:658
  88.8 2.1 %shard_map.94 = (bf16[384,1408]{1,0:T(8,128)(2,1)}, bf16[384,1408]{1,0:T(8,128)(2,1)}, bf16[768,1408]{1,0:T(8,128)(2,1)}, f32[4,64]{1,0:T(4,128)}) custom-call(bf16[384,1408]{1,0:T(8,128)(2,1)S(1)} %get-tuple-element.12.refs_0_, bf16[384,1408]{1,0:T(8,128)(2,1)S(1)} %get-tuple-element.13.refs_1_, bf16[768,1408]{1,0:T(8,128)(2,1)S(1)} %get-tuple-element.14.refs_2_, ...), custom_call_target="tpu_custom_call" | custom-call | tf_op jit(solution)/shard_map/pallas_call | solution.py:716

commit v3 on v2

--- a/solution.py
+++ b/solution.py
@@ -17,6 +17,10 @@
     return pltpu.make_async_copy(src, dst, sem)
 
 
+def landed(ref, sem):
+    pltpu.make_async_copy(ref, ref, sem).wait()
+
+
 def silu_factors(gate_value, up_value):
     sigmoid_gate = jax.nn.sigmoid(gate_value)
     activated = gate_value * sigmoid_gate
@@ -27,9 +31,9 @@
 def kernel(
     experts, cap, tok, top,
     og, ids, probs, gate, up, w,
-    gate_out, up_out, wg_out, router_out,
-    ids_ref, probs_ref, og_v, gate_v, up_v, w_v, a_gate, a_up, hid, rows, x2, meta_own, meta_in, sb,
-    part_f, part_b, sb_c, rb_o, rb_d, rb_c, wg_acc,
+    a_gate, a_up, wg_acc, late_rows, late_hid, scales, router_out,
+    ids_ref, probs_ref, og_v, gate_v, up_v, w_v, hid, rows, x2, meta_own, meta_in, sb,
+    part_f, part_b, sb_c, rb_o, rb_d, rb_c,
     pk_own, pk_in, pk_row, pk_rows, rl, rz_out, rz_in, ry_own, ry_in,
     load_sem, xs, xr, ms, mr, zs, zr, ys, yr, hs, hr, bs, br, ps, pr, qs, qr, ws, wr, vs, vr,
 ):
@@ -44,6 +48,8 @@
     x_right, x_left, x_far = lax.rem(x + 1, RING), lax.rem(x + 3, RING), lax.rem(x + 2, RING)
     y_right, y_left, y_far = lax.rem(y + 1, RING), lax.rem(y + 3, RING), lax.rem(y + 2, RING)
     first, second = pl.ds(0, half), pl.ds(half, half)
+    fill_right = jnp.logical_or(x == y, x_left == y)
+    fill_left = jnp.logical_or(x == y, x_right == y)
 
     def share(core):
         return lax.rem(y - x + 2 * core + RING, RING)
@@ -53,30 +59,31 @@
     takes_home = jnp.logical_and(from_y == y, x == y)
     stays = jnp.logical_and(share(c) == x, x == y)
 
-    loads = []
-    for i, part in enumerate((first, second)):
-        loads.append((
-            local(gate.at[part], gate_v.at[part], load_sem.at[2 * i]),
-            local(up.at[part], up_v.at[part], load_sem.at[2 * i + 1]),
-        ))
-    load_w = local(w, w_v, load_sem.at[4])
+    loads = [
+        tuple(
+            local(ref.at[part], held.at[part], load_sem.at[6 + 2 * i + k])
+            for k, (ref, held) in enumerate(((gate, gate_v), (up, up_v)))
+        )
+        for i, part in enumerate((first, second))
+    ]
+    load_w = local(w, w_v, load_sem.at[2])
     small = (
-        local(ids, ids_ref, load_sem.at[5]),
-        local(probs, probs_ref, load_sem.at[6]),
-    ) + tuple(
+        local(ids, ids_ref, load_sem.at[3]),
+        local(probs, probs_ref, load_sem.at[4]),
+    )
+    tokens = tuple(
         local(
             og.at[:, pl.ds(
                 pl.multiple_of(features * share(core) + lanes_half * core, 128), lanes_half
             )],
-            og_v.at[core], load_sem.at[7 + core],
+            og_v.at[core], load_sem.at[5],
         )
         for core in range(2)
     )
-    for copy in small:
+    for copy in small + tokens:
         copy.start()
-    for pair_of in loads:
-        for copy in pair_of:
-            copy.start()
+    for copy in loads[0] + loads[1]:
+        copy.start()
     load_w.start()
 
     barrier = pltpu.get_barrier_semaphore()
@@ -112,7 +119,7 @@
     )
     meta_own[4:4 + top, :] = jnp.dot(probs_ref[...], place, preferred_element_type=F32)
 
-    for i in range(2):
+    def hidden_of(i):
         for copy in loads[i]:
             copy.wait()
 
@@ -128,6 +135,8 @@
                 a_gate[part, lanes] = gate_factor
                 a_up[part, lanes] = up_factor
 
+    landed(og_v, load_sem.at[5])
+    hidden_of(0)
     peers = experts - 1 + RING * RING - 1
     pl.semaphore_wait(barrier, peers + jnp.where(gives_home, 0, 1) + jnp.where(takes_home, 0, 1))
 
@@ -158,29 +167,32 @@
                 copy.start()
 
     part_a, part_e = pl.ds(0, quarter), pl.ds(quarter, quarter)
-    eighth = quarter // 2
-    part_c, part_d = pl.ds(quarter, eighth), pl.ds(quarter + eighth, eighth)
+    last = quarter // 3
+    more = quarter - last
+    part_c, part_d = pl.ds(quarter, more), pl.ds(quarter + more, last)
     far_a = pl.ds(half, quarter)
-    far_c, far_d = (pl.ds(half + quarter + i * eighth, eighth) for i in range(2))
+    far_c, far_d = pl.ds(half + quarter, more), pl.ds(half + quarter + more, last)
 
     def pass_hidden(index, block, part, to_right):
         at = hid.at[block, part]
         return pltpu.make_async_remote_copy(
-            src_ref=at, dst_ref=at, send_sem=hs.at[index], recv_sem=hr.at[index],
+            src_ref=at, dst_ref=at, send_sem=hs.at[0], recv_sem=hr.at[index],
             device_id=(e, x_right if to_right else x_left, y), device_id_type=MESH,
         )
 
     h_r0 = pass_hidden(0, x, first, True)
-    h_r1 = pass_hidden(1, x, second, True)
+    h_r1 = pass_hidden(2, x, second, True)
     h_l0 = pass_hidden(2, x, first, False)
-    h_l1 = pass_hidden(3, x, second, False)
-    h_ra = pass_hidden(4, x_left, part_a, True)
-    h_la = pass_hidden(5, x_right, far_a, False)
-    h_rc = pass_hidden(6, x_left, part_c, True)
-    h_lc = pass_hidden(7, x_right, far_c, False)
-    h_rd = pass_hidden(8, x_left, part_d, True)
-    h_ld = pass_hidden(9, x_right, far_d, False)
-    for copy in (h_r0, h_l1, h_r1, h_l0):
+    h_l1 = pass_hidden(1, x, second, False)
+    h_ra = pass_hidden(3, x_left, part_a, True)
+    h_la = pass_hidden(3, x_right, far_a, False)
+    h_rc = pass_hidden(4, x_left, part_c, True)
+    h_lc = pass_hidden(4, x_right, far_c, False)
+    h_rd = pass_hidden(5, x_left, part_d, True)
+    h_ld = pass_hidden(5, x_right, far_d, False)
+    h_r0.start()
+    hidden_of(1)
+    for copy in (h_l1, h_r1, h_l0):
         copy.start()
     for core in range(2):
         local(meta_own, meta_in.at[core], mr.at[core]).wait()
@@ -218,7 +230,7 @@
         return pltpu.make_async_remote_copy(
             src_ref=sb.at[pl.ds(pl.multiple_of(pair * to, 16), pair)],
             dst_ref=rows.at[y, my_rows, my_lanes],
-            send_sem=zs.at[to], recv_sem=zr.at[e],
+            send_sem=zs.at[0], recv_sem=zr.at[z],
             device_id=(to, x, y), device_id_type=MESH,
         )
 
@@ -229,7 +241,7 @@
         return lax.rem(jnp.where(lax.rem(j, 2) == 1, z + away, z - away + chips), chips)
 
     local(
-        sb.at[pl.ds(pl.multiple_of(pair * e, 16), pair)], rows.at[y, my_rows, my_lanes], zr.at[e]
+        sb.at[pl.ds(pl.multiple_of(pair * e, 16), pair)], rows.at[y, my_rows, my_lanes], zr.at[z]
     ).start()
     dispatch(2 * z + 1 - c).start()
 
@@ -241,10 +253,10 @@
     def _(j):
         dispatch_both(j)
 
-    def pass_rows(j, block, to_right, index):
+    def pass_rows(j, block, to_right, sem):
         at = rows.at[block, pl.ds(pl.multiple_of(pair * chip(j), 16), pair)]
         return pltpu.make_async_remote_copy(
-            src_ref=at, dst_ref=at, send_sem=ys.at[index], recv_sem=yr.at[index],
+            src_ref=at, dst_ref=at, send_sem=ys.at[0], recv_sem=yr.at[sem],
             device_id=(e, x, y_right if to_right else y_left), device_id_type=MESH,
         )
 
@@ -252,27 +264,23 @@
         return pass_rows(j, y, True, j)
 
     def go_left(j):
-        return pass_rows(j, y, False, chips + j)
+        return pass_rows(j, y, False, j)
 
     def on_right(j):
-        return pass_rows(j, y_left, True, 2 * chips + j)
+        return pass_rows(j, y_left, True, chips)
 
     def on_left(j):
-        return pass_rows(j, y_right, False, 2 * chips + j)
+        return pass_rows(j, y_right, False, chips)
 
     def start_own(j):
-        for core in range(2):
-            at = rows.at[
-                y, pl.ds(pl.multiple_of(pair * chip(j), 16), pair),
-                pl.ds(lanes_half * core, lanes_half),
-            ]
-            local(at, at, zr.at[2 * chip(j) + core]).wait()
+        landed(
+            rows.at[y, pl.ds(pl.multiple_of(pair * chip(j), 16), pair)], zr.at[chip(j)]
+        )
         go_right(j).start()
         go_left(j).start()
 
     def start_on(j):
-        go_right(j).wait_recv()
-        go_left(j).wait_recv()
+        landed(rows.at[pl.ds(0, 2), pl.ds(0, pair)], yr.at[j])
 
         (on_right, on_left)[j % 2](j).start()
 
@@ -280,7 +288,7 @@
 
     def send(index, src, dst, to_right):
         return pltpu.make_async_remote_copy(
-            src_ref=src, dst_ref=dst, send_sem=bs.at[index], recv_sem=br.at[index],
+            src_ref=src, dst_ref=dst, send_sem=bs.at[0], recv_sem=br.at[index],
             device_id=(e, x_right if to_right else x_left, y), device_id_type=MESH,
         )
 
@@ -288,14 +296,14 @@
     far1 = send(1, part_b.at[2, 1], rb_o.at[1], False)
     near0, near1 = (
         [
-            send(8 + 2 * i + k, part_b.at[role, 1 - k, part], rb_d.at[k, part], k == 0)
-            for i, part in enumerate((part_a, part_e))
+            send(2, part_b.at[role, 1 - k, part], rb_d.at[k, part], k == 0)
+            for part in (part_a, part_e)
         ]
         for k, role in enumerate((1, 3))
     )
     both = [
-        (send(4 + 2 * i, sb_c.at[0, part], rb_c.at[0, part], True),
-         send(5 + 2 * i, sb_c.at[1, part], rb_c.at[1, part], False))
+        (send(3 + i, sb_c.at[0, part], rb_c.at[0, part], True),
+         send(3 + i, sb_c.at[1, part], rb_c.at[1, part], False))
         for i, part in enumerate((part_a, part_e))
     ]
 
@@ -325,10 +333,13 @@
     for j in range(chips):
         start_own(j)
 
-    @pl.when(x == y)
+    @pl.when(fill_right)
     def _():
         h_r0.wait_recv()
         h_rc.start()
+
+    @pl.when(fill_left)
+    def _():
         h_l1.wait_recv()
         h_lc.start()
 
@@ -341,27 +352,20 @@
     partial(jnp.where(x == y_right, y_left, y_right))
     partial(jnp.where(x == y_right, y_right, y_left))
 
-    @pl.loop(0, chips)
-    def _(j):
-        @pl.when(lax.rem(j, 2) == 0)
-        def _():
-            on_right(j).wait_recv()
-
-        @pl.when(lax.rem(j, 2) == 1)
-        def _():
-            on_left(j).wait_recv()
-
+    landed(rows.at[y_far], yr.at[chips])
     partial(y_far)
     near0[1].start()
     near1[1].start()
 
-    @pl.when(x != y)
+    @pl.when(jnp.logical_not(fill_right))
     def _():
         h_r0.wait_recv()
+
+    @pl.when(jnp.logical_not(fill_left))
+    def _():
         h_l1.wait_recv()
 
-    for copy in (h_r1, h_l0):
-        copy.wait_recv()
+    landed(hid.at[x], hr.at[2])
     step = 256 if features % 256 == 0 else 128
 
     def outer(block, slot_parts, at):
@@ -377,10 +381,8 @@
             outer(x, everything, at) + outer(x_left, everything, at) + outer(x_right, everything, at)
         )
     early = (slice(0, quarter), slice(half, half + quarter))
-    late = [
-        tuple(slice(at + i * eighth, at + (i + 1) * eighth) for at in (quarter, half + quarter))
-        for i in range(2)
-    ]
+    late = tuple(slice(at, at + more) for at in (quarter, half + quarter))
+    latest = tuple(slice(at + more, at + quarter) for at in (quarter, half + quarter))
 
     for core in range(2):
         @pl.when(jnp.logical_not(jnp.logical_and(stays, c == core)))
@@ -388,22 +390,8 @@
             for copy in swap(core):
                 copy.wait_send()
 
-    @pl.loop(1, experts)
-    def _(i):
-        dispatch(lax.rem(e + i, experts)).wait_send()
-
-    @pl.loop(0, chips)
-    def _(j):
-        go_right(j).wait_send()
-        go_left(j).wait_send()
-
-        @pl.when(lax.rem(j, 2) == 0)
-        def _():
-            on_right(j).wait_send()
-
-        @pl.when(lax.rem(j, 2) == 1)
-        def _():
-            on_left(j).wait_send()
+    landed(sb.at[pl.ds(0, pair * (experts - 1))], zs.at[0])
+    landed(rows.at[pl.ds(0, 3)], ys.at[0])
 
     def pass_on(side):
         @pl.when(side == 0)
@@ -427,33 +415,27 @@
                 def _():
                     both[i][k].start()
 
-        @pl.when(side == 0)
-        def _():
-            h_ra.start()
-
-        @pl.when(side == 1)
-        def _():
-            h_la.start()
-
-        @pl.when(jnp.logical_and(side == 0, x != y))
-        def _():
-            h_rc.start()
-
-        @pl.when(jnp.logical_and(side == 1, x != y))
-        def _():
-            h_lc.start()
-
     early_side = jnp.where(x_left == y, 1, 0)
     pass_on(early_side)
     pass_on(1 - early_side)
-    for copy in near0 + near1:
-        copy.wait_recv()
+
+    h_ra.start()
+    h_la.start()
+
+    @pl.when(jnp.logical_not(fill_right))
+    def _():
+        h_rc.start()
+
+    @pl.when(jnp.logical_not(fill_left))
+    def _():
+        h_lc.start()
+
+    landed(rb_d, br.at[2])
 
     zero = jnp.zeros((16, 128), F32)
     peaks = (zero, zero)
-    for i, pair_of in enumerate(both):
-        for copy in pair_of:
-            copy.wait_recv()
+    for i in range(2):
+        landed(rb_c.at[pl.ds(0, 2), pl.ds(0, quarter)], br.at[3 + i])
         for side in range(2):
             def body(j, carry):
                 gate_peak, up_peak = carry
@@ -484,13 +466,13 @@
 
     def tell_row(p):
         return pltpu.make_async_remote_copy(
-            src_ref=pk_own, dst_ref=pk_in.at[y], send_sem=ps.at[p], recv_sem=pr.at[y],
+            src_ref=pk_own, dst_ref=pk_in.at[y], send_sem=ps.at[0], recv_sem=pr.at[0],
             device_id=(e, x, p), device_id_type=MESH,
         )
 
     def tell_column(p):
         return pltpu.make_async_remote_copy(
-            src_ref=pk_row, dst_ref=pk_rows.at[x], send_sem=qs.at[p], recv_sem=qr.at[x],
+            src_ref=pk_row, dst_ref=pk_rows.at[x], send_sem=qs.at[0], recv_sem=qr.at[0],
             device_id=(e, p, y), device_id_type=MESH,
         )
 
@@ -513,7 +495,7 @@
 
     def give_back(to):
         return pltpu.make_async_remote_copy(
-            src_ref=rz_out, dst_ref=rz_in.at[e], send_sem=ws.at[to], recv_sem=wr.at[e],
+            src_ref=rz_out, dst_ref=rz_in.at[e], send_sem=ws.at[0], recv_sem=wr.at[0],
             device_id=(to, x, y), device_id_type=MESH,
         )
 
@@ -523,19 +505,15 @@
 
     rz_in[e] = rz_out[...]
     row_peak = pk_own[...]
+    landed(pk_in.at[pl.ds(0, 3)], pr.at[0])
     for p in y_others:
-        local(pk_in.at[p], pk_in.at[p], pr.at[p]).wait()
         row_peak = jnp.maximum(row_peak, pk_in[p])
     pk_row[...] = row_peak
     for p in x_others:
         tell_column(p).start()
     h_rd.start()
     h_ld.start()
-    @pl.loop(1, experts)
-    def _(i):
-        s = lax.rem(e + i, experts)
-        local(rz_in.at[s], rz_in.at[s], wr.at[s]).wait()
-
+    landed(rz_in.at[pl.ds(0, experts - 1)], wr.at[0])
     from_experts = rz_in[:, 0, :]
     mine = (
         lax.broadcasted_iota(jnp.int32, (128, from_experts.shape[1]), 1)
@@ -548,36 +526,31 @@
 
     def tell_sum(p):
         return pltpu.make_async_remote_copy(
-            src_ref=ry_own, dst_ref=ry_in.at[y], send_sem=vs.at[p], recv_sem=vr.at[y],
+            src_ref=ry_own, dst_ref=ry_in.at[y], send_sem=vs.at[0], recv_sem=vr.at[0],
             device_id=(e, x, p), device_id_type=MESH,
         )
 
     for p in y_others:
         tell_sum(p).start()
 
-    for copy in (h_ra, h_la):
-        copy.wait_recv()
+    landed(hid.at[x_far, pl.ds(0, 2 * quarter)], hr.at[3])
     for at in range(0, features, step):
         wg_acc[at:at + step, :] += outer(x_far, early, at)
 
     all_peaks = row_peak
+    landed(pk_rows.at[pl.ds(0, 3)], qr.at[0])
     for p in x_others:
-        local(pk_rows.at[p], pk_rows.at[p], qr.at[p]).wait()
         all_peaks = jnp.maximum(all_peaks, pk_rows[p])
-    gate_scale = 1.0 / (jnp.max(all_peaks[:4], axis=(0, 1), keepdims=True) + 1e-6)
-    up_scale = 1.0 / (jnp.max(all_peaks[4:], axis=(0, 1), keepdims=True) + 1e-6)
-
-    @pl.loop(0, slots // 16)
-    def _(j):
-        part = pl.ds(pl.multiple_of(j * 16, 16), 16)
-        gate_out[part, :] = (a_gate[part, :] * gate_scale).astype(BF16)
-        up_out[part, :] = (a_up[part, :] * up_scale).astype(BF16)
-
-    for copy in (h_rc, h_lc):
-        copy.wait_recv()
+    scales[...] = 1.0 / (
+        jnp.where(
+            peak_row < 4,
+            jnp.max(all_peaks[:4], axis=(0, 1), keepdims=True),
+            jnp.max(all_peaks[4:], axis=(0, 1), keepdims=True),
+        ) + 1e-6
+    )
+    landed(hid.at[x_far, pl.ds(0, 2 * more)], hr.at[4])
     for at in range(0, features, step):
-        wg_acc[at:at + step, :] += outer(x_far, late[0], at)
-
+        wg_acc[at:at + step, :] += outer(x_far, late, at)
 
     ids_f = ids_ref[...].astype(F32)
     expert_col = lax.broadcasted_iota(jnp.int32, (experts, tok), 0).astype(F32)
@@ -591,8 +564,7 @@
     at_slot = [
         slot_col == jnp.sum(earlier * named[k], axis=0, keepdims=True) for k in range(top)
     ]
-    for p in y_others:
-        local(ry_in.at[p], ry_in.at[p], vr.at[p]).wait()
+    landed(ry_in.at[pl.ds(0, 3)], vr.at[0])
     sums = ry_own[...]
     for p in y_others:
         sums = sums + ry_in[p]
@@ -606,35 +578,50 @@
         value = jnp.sum(jnp.where(at_slot[k], found, 0.0), axis=0, keepdims=True)
         router_out[k:k + 1, :] = value / probs_ref[k:k + 1, :].astype(F32)
 
-    for copy in (h_rd, h_ld):
-        copy.wait_recv()
+    landed(hid.at[x_far, pl.ds(0, 2 * last)], hr.at[5])
+    late_rows[...] = jnp.concatenate([rows[x_far, p, :] for p in latest], axis=0)
+    late_hid[...] = jnp.concatenate([hid[x_far, p, :] for p in latest], axis=0)
+
+    landed(rz_in.at[pl.ds(0, experts - 1)], ws.at[0])
+    landed(ry_in.at[pl.ds(0, 3)], vs.at[0])
+    landed(pk_in.at[pl.ds(0, 3)], ps.at[0])
+    landed(pk_rows.at[pl.ds(0, 3)], qs.at[0])
+    landed(hid.at[pl.ds(0, 3)], hs.at[0])
+    landed(part_b.at[pl.ds(0, 3)], bs.at[0])
+
+
+def finish(
+    a_gate, a_up, wg_acc, late_rows, late_hid, scales, router, gate_out, up_out, wg_out, router_out,
+    gate_v, up_v, wg_v, sem,
+):
+    local(router, router_out, sem.at[3]).start()
+
+    def write(source, target, part, k):
+        local(source.at[part], target.at[part], sem.at[k]).start()
+
+    slots, features = a_gate.shape[0], wg_acc.shape[0]
+    step = 128
     for at in range(0, features, step):
-        wg_out[at:at + step, :] = (wg_acc[at:at + step, :] + outer(x_far, late[1], at)).astype(BF16)
-
-    @pl.loop(1, experts)
-    def _(i):
-        to = lax.rem(e + i, experts)
-        give_back(to).wait_send()
-
-    for p in y_others:
-        tell_sum(p).wait_send()
-        tell_row(p).wait_send()
-    for p in x_others:
-        tell_column(p).wait_send()
-    for copy in (h_r0, h_r1, h_l0, h_l1, h_ra, h_la, h_rc, h_lc, h_rd, h_ld):
-        copy.wait_send()
-
-    for copy in [far0, far1] + near0 + near1 + list(both[0] + both[1]):
-        copy.wait_send()
-
-
-def write_out(*refs):
-    count = len(refs) // 2
-    copies = [local(refs[i], refs[count + i], refs[-1].at[i]) for i in range(count)]
-    for copy in copies:
-        copy.start()
-    for copy in copies:
-        copy.wait()
+        wg_v[at:at + step, :] = (
+            wg_acc[at:at + step, :] + lax.dot_general(
+                late_rows[:, at:at + step], late_hid[...], (((0,), (0,)), ((), ())),
+                preferred_element_type=F32,
+            )
+        ).astype(BF16)
+        write(wg_v, wg_out, pl.ds(at, step), 2)
+    size = slots // 4
+    for at in range(0, slots, size):
+        for k, delta, staged, out in ((0, a_gate, gate_v, gate_out), (1, a_up, up_v, up_out)):
+            factor = scales[4 * k:4 * k + 1, 0:1]
+
+            @pl.loop(0, size // 32)
+            def _(j):
+                part = pl.ds(pl.multiple_of(at + j * 32, 32), 32)
+                staged[part, :] = (delta[part, :] * factor).astype(BF16)
+
+            write(staged, out, pl.ds(at, size), k)
+    for k, out in enumerate((gate_out, up_out, wg_out, router_out)):
+        landed(out, sem.at[k])
 
 
 def shards(out_grad, router_probs, expert_ids, saved_gate, saved_up, down_weight):
@@ -655,11 +642,16 @@
         ((slots, width), BF16), ((slots, width), BF16), ((features, width), BF16),
         ((top, tok), F32),
     )
+    last = half // 3
+    between = (
+        ((slots, width), F32), ((slots, width), F32), ((features, width), F32),
+        ((last, features), BF16), ((last, width), BF16), ((8, 128), F32), ((top, tok), F32),
+    )
     results = pl.pallas_call(
         functools.partial(kernel, experts, cap, tok, top),
-        out_shape=tuple(pltpu.VMEM(*shape) for shape in shapes),
+        out_shape=tuple(pltpu.VMEM(*shape) for shape in between),
         in_specs=[hbm] * 6,
-        out_specs=(vmem,) * 4,
+        out_specs=(vmem,) * len(between),
         scratch_shapes=[
             pltpu.VMEM((top, tok), jnp.int32),
             pltpu.VMEM((top, tok), BF16),
@@ -667,8 +659,6 @@
             pltpu.VMEM((slots, width), BF16),
             pltpu.VMEM((slots, width), BF16),
             pltpu.VMEM((features, width), BF16),
-            pltpu.VMEM((slots, width), F32),
-            pltpu.VMEM((slots, width), F32),
             pltpu.VMEM((RING, slots, width), BF16),
             pltpu.VMEM((RING, slots, features), BF16),
             pltpu.VMEM((2, tok, features // 2), BF16),
@@ -681,7 +671,6 @@
             pltpu.VMEM((2, half, width), BF16),
             pltpu.VMEM((2, half, width), BF16),
             pltpu.VMEM((2, half, width), BF16),
-            pltpu.VMEM((features, width), F32),
             pltpu.VMEM((8, 128), F32),
             pltpu.VMEM((RING, 8, 128), F32),
             pltpu.VMEM((8, 128), F32),
@@ -691,18 +680,18 @@
             pltpu.VMEM((experts, 1, slots + 128), F32),
             pltpu.VMEM((experts, 128), F32),
             pltpu.VMEM((RING, experts, 128), F32),
-            dma((9,)),
+            dma((10,)),
             dma((2,)), dma((2,)), dma((2,)), dma((2,)),
-            dma((experts,)), dma((experts,)),
-            dma((3 * chips,)), dma((3 * chips,)),
-            dma((10,)), dma((10,)),
-            dma((12,)), dma((12,)),
-            dma((RING,)), dma((RING,)), dma((RING,)), dma((RING,)),
-            dma((experts,)), dma((experts,)),
-            dma((RING,)), dma((RING,)),
+            dma((1,)), dma((chips,)),
+            dma((1,)), dma((chips + 1,)),
+            dma((1,)), dma((6,)),
+            dma((1,)), dma((5,)),
+            dma((1,)), dma((1,)), dma((1,)), dma((1,)),
+            dma((1,)), dma((1,)),
+            dma((1,)), dma((1,)),
         ],
         compiler_params=pltpu.CompilerParams(
-            collective_id=0, has_side_effects=True, vmem_limit_bytes=48 * 1024 * 1024
+            collective_id=0, has_side_effects=True, vmem_limit_bytes=40 * 1024 * 1024
         ),
         cost_estimate=pl.CostEstimate(
             flops=4 * RING * slots * features * width,
@@ -714,12 +703,12 @@
         stay(saved_up.reshape(slots, width)), stay(down_weight.reshape(features, width)),
     )
     gate_grad, up_grad, weight_grad, router_grad = pl.pallas_call(
-        write_out,
+        finish,
         out_shape=tuple(jax.ShapeDtypeStruct(*shape) for shape in shapes),
-        in_specs=[vmem] * 4,
+        in_specs=[vmem] * len(between),
         out_specs=(any_space,) * 4,
-        scratch_shapes=[dma((4,))],
-        compiler_params=pltpu.CompilerParams(vmem_limit_bytes=1024 * 1024),
+        scratch_shapes=[pltpu.VMEM(*shape) for shape in shapes[:3]] + [dma((4,))],
+        compiler_params=pltpu.CompilerParams(vmem_limit_bytes=8 * 1024 * 1024),
     )(*(pltpu.with_memory_space_constraint(r, memory_space=pltpu.VMEM) for r in results))
     return (
         gate_grad.reshape(saved_gate.shape), up_grad.reshape(saved_up.shape),

time: 91 us -> 89.6 us (0.985)
  Pallas kernels: 90.3 us -> 88.9 us
    pallas_call x1, Pallas kernels: 88.2 us -> 86.3 us  [shards(): pl.pallas_call(functools.partial(kernel, experts, cap, tok, top), out_sha...]
where the time goes in v3:
time: 89.6 us; the launch traced here: 89.5 us
  Pallas kernels  88.9 us (99%)
    pallas_call x1, Pallas kernels, shards(): pl.pallas_call(functools.partial(kernel, experts, cap, tok, top), out_sha...  86.3 us
    pallas_call x1, Pallas kernels, shards(): pl.pallas_call(finish, out_shape=tuple((jax.ShapeDtypeStruct(*shape) for...  2.63 us

profile of v3, /device:TPU:1, one launch (start us, length us, event | category | flops | bytes accessed | tf_op | source)
XLA Modules:
  0.0 89.5 jit_solution(13483232041950920728)
XLA Ops:
  0.6 86.3 %shard_map.93 = (f32[384,1408]{1,0:T(8,128)S(1)}, f32[384,1408]{1,0:T(8,128)S(1)}, f32[768,1408]{1,0:T(8,128)S(1)}, bf16[64,768]{1,0:T(8,128)(2,1)S(1)}, bf16[64...) custom-call(bf16[64,3072]{1,0:T(8,128)(2,1)} %og.1, s32[4,64]{1,0:T(4,128)} %bitcast.15, ...), custom_call_target="tpu_custom_call" | custom-call | flops 6643777536 | bytes 4325376 | tf_op jit(solution)/shard_map/pallas_call | solution.py:650
  86.9 2.6 %shard_map.94 = (bf16[384,1408]{1,0:T(8,128)(2,1)}, bf16[384,1408]{1,0:T(8,128)(2,1)}, bf16[768,1408]{1,0:T(8,128)(2,1)}, f32[4,64]{1,0:T(4,128)}) custom-call(f32[384,1408]{1,0:T(8,128)S(1)} %get-tuple-element.15.a_gate, f32[384,1408]{1,0:T(8,128)S(1)} %get-tuple-element.16.a_up, f32[768,1408]{1,0:T(8,128)S(1)} %get-tuple-element.17.wg_acc, ...), custom_call_target="tpu_custom_call" | custom-call | tf_op jit(solution)/shard_map/pallas_call | solution.py:705

commit v4 on v3

--- a/solution.py
+++ b/solution.py
@@ -48,8 +48,8 @@
     x_right, x_left, x_far = lax.rem(x + 1, RING), lax.rem(x + 3, RING), lax.rem(x + 2, RING)
     y_right, y_left, y_far = lax.rem(y + 1, RING), lax.rem(y + 3, RING), lax.rem(y + 2, RING)
     first, second = pl.ds(0, half), pl.ds(half, half)
-    fill_right = jnp.logical_or(x == y, x_left == y)
-    fill_left = jnp.logical_or(x == y, x_right == y)
+    fill_right = x == y
+    fill_left = x == y
 
     def share(core):
         return lax.rem(y - x + 2 * core + RING, RING)
@@ -58,6 +58,37 @@
     gives_home = jnp.logical_and(share(1 - c) == x, x == y)
     takes_home = jnp.logical_and(from_y == y, x == y)
     stays = jnp.logical_and(share(c) == x, x == y)
+    gives_near = jnp.logical_or(share(c) == x, x == y)
+    takes_near = jnp.logical_or(from_y == y, x == y)
+
+    barrier = pltpu.get_barrier_semaphore()
+
+    def greet(device):
+        pl.semaphore_signal(barrier, inc=1, device_id=device, device_id_type=MESH)
+
+    @pl.loop(1, experts)
+    def _(i):
+        greet((lax.rem(e + i, experts), x, y))
+
+    for i in range(1, RING):
+        greet((e, lax.rem(x + i, RING), y))
+        greet((e, x, lax.rem(y + i, RING)))
+
+    @pl.when(jnp.logical_not(gives_near))
+    def _():
+        greet((e, share(c), x))
+
+    @pl.when(jnp.logical_not(takes_near))
+    def _():
+        greet((e, y, from_y))
+
+    @pl.when(jnp.logical_not(gives_home))
+    def _():
+        greet((2 * z + 1 - c, share(1 - c), x))
+
+    @pl.when(jnp.logical_not(takes_home))
+    def _():
+        greet((2 * z + 1 - c, y, from_y))
 
     loads = [
         tuple(
@@ -85,28 +116,6 @@
     for copy in loads[0] + loads[1]:
         copy.start()
     load_w.start()
-
-    barrier = pltpu.get_barrier_semaphore()
-
-    def greet(device):
-        pl.semaphore_signal(barrier, inc=1, device_id=device, device_id_type=MESH)
-
-    @pl.loop(1, experts)
-    def _(i):
-        greet((lax.rem(e + i, experts), x, y))
-
-    @pl.loop(1, RING * RING)
-    def _(i):
-        p = lax.rem(x * RING + y + i, RING * RING)
-        greet((e, lax.div(p, RING), lax.rem(p, RING)))
-
-    @pl.when(jnp.logical_not(gives_home))
-    def _():
-        greet((2 * z + 1 - c, share(1 - c), x))
-
-    @pl.when(jnp.logical_not(takes_home))
-    def _():
-        greet((2 * z + 1 - c, y, from_y))
 
     place = (
         lax.broadcasted_iota(jnp.int32, (tok, 128), 1)
@@ -137,8 +146,10 @@
 
     landed(og_v, load_sem.at[5])
     hidden_of(0)
-    peers = experts - 1 + RING * RING - 1
-    pl.semaphore_wait(barrier, peers + jnp.where(gives_home, 0, 1) + jnp.where(takes_home, 0, 1))
+    peers = experts - 1 + 2 * (RING - 1)
+    for near in (gives_near, takes_near, gives_home, takes_home):
+        peers = peers + jnp.where(near, 0, 1)
+    pl.semaphore_wait(barrier, peers)
 
     def swap(core):
         device = (2 * z + core, share(core), x)

time: 89.6 us -> 88.8 us (level)
  no operation moved by 1% of the time
where the time goes in v4:
time: 88.8 us; the launch traced here: 88.7 us
  Pallas kernels  88.1 us (99%)
    pallas_call x1, Pallas kernels, shards(): pl.pallas_call(functools.partial(kernel, experts, cap, tok, top), out_sha...  85.5 us
    pallas_call x1, Pallas kernels, shards(): pl.pallas_call(finish, out_shape=tuple((jax.ShapeDtypeStruct(*shape) for...  2.63 us

profile of v4, /device:TPU:1, one launch (start us, length us, event | category | flops | bytes accessed | tf_op | source)
XLA Modules:
  0.0 88.7 jit_solution(17082120876910423153)
XLA Ops:
  0.6 85.5 %shard_map.93 = (f32[384,1408]{1,0:T(8,128)S(1)}, f32[384,1408]{1,0:T(8,128)S(1)}, f32[768,1408]{1,0:T(8,128)S(1)}, bf16[64,768]{1,0:T(8,128)(2,1)S(1)}, bf16[64...) custom-call(bf16[64,3072]{1,0:T(8,128)(2,1)} %og.1, s32[4,64]{1,0:T(4,128)} %bitcast.15, ...), custom_call_target="tpu_custom_call" | custom-call | flops 6643777536 | bytes 4325376 | tf_op jit(solution)/shard_map/pallas_call | solution.py:661
  86.1 2.6 %shard_map.94 = (bf16[384,1408]{1,0:T(8,128)(2,1)}, bf16[384,1408]{1,0:T(8,128)(2,1)}, bf16[768,1408]{1,0:T(8,128)(2,1)}, f32[4,64]{1,0:T(4,128)}) custom-call(f32[384,1408]{1,0:T(8,128)S(1)} %get-tuple-element.15.a_gate, f32[384,1408]{1,0:T(8,128)S(1)} %get-tuple-element.16.a_up, f32[768,1408]{1,0:T(8,128)S(1)} %get-tuple-element.17.wg_acc, ...), custom_call_target="tpu_custom_call" | custom-call | tf_op jit(solution)/shard_map/pallas_call | solution.py:716

commit v5 on v4

--- a/solution.py
+++ b/solution.py
@@ -178,7 +178,7 @@
                 copy.start()
 
     part_a, part_e = pl.ds(0, quarter), pl.ds(quarter, quarter)
-    last = quarter // 3
+    last = quarter // 2
     more = quarter - last
     part_c, part_d = pl.ds(quarter, more), pl.ds(quarter + more, last)
     far_a = pl.ds(half, quarter)
@@ -653,7 +653,7 @@
         ((slots, width), BF16), ((slots, width), BF16), ((features, width), BF16),
         ((top, tok), F32),
     )
-    last = half // 3
+    last = half // 2
     between = (
         ((slots, width), F32), ((slots, width), F32), ((features, width), F32),
         ((last, features), BF16), ((last, width), BF16), ((8, 128), F32), ((top, tok), F32),

time: 88.8 us -> 88.3 us (level)
  Pallas kernels: 88.1 us -> 87.2 us
where the time goes in v5:
time: 88.3 us; the launch traced here: 87.9 us
  Pallas kernels  87.2 us (99%)
    pallas_call x1, Pallas kernels, shards(): pl.pallas_call(functools.partial(kernel, experts, cap, tok, top), out_sha...  84.6 us
    pallas_call x1, Pallas kernels, shards(): pl.pallas_call(finish, out_shape=tuple((jax.ShapeDtypeStruct(*shape) for...  2.64 us

profile of v5, /device:TPU:1, one launch (start us, length us, event | category | flops | bytes accessed | tf_op | source)
XLA Modules:
  0.0 87.9 jit_solution(18275888090462748877)
XLA Ops:
  0.6 84.6 %shard_map.93 = (f32[384,1408]{1,0:T(8,128)S(1)}, f32[384,1408]{1,0:T(8,128)S(1)}, f32[768,1408]{1,0:T(8,128)S(1)}, bf16[96,768]{1,0:T(8,128)(2,1)S(1)}, bf16[96...) custom-call(bf16[64,3072]{1,0:T(8,128)(2,1)} %og.1, s32[4,64]{1,0:T(4,128)} %bitcast.15, ...), custom_call_target="tpu_custom_call" | custom-call | flops 6643777536 | bytes 4325376 | tf_op jit(solution)/shard_map/pallas_call | solution.py:661
  85.2 2.6 %shard_map.94 = (bf16[384,1408]{1,0:T(8,128)(2,1)}, bf16[384,1408]{1,0:T(8,128)(2,1)}, bf16[768,1408]{1,0:T(8,128)(2,1)}, f32[4,64]{1,0:T(4,128)}) custom-call(f32[384,1408]{1,0:T(8,128)S(1)} %get-tuple-element.15.a_gate, f32[384,1408]{1,0:T(8,128)S(1)} %get-tuple-element.16.a_up, f32[768,1408]{1,0:T(8,128)S(1)} %get-tuple-element.17.wg_acc, ...), custom_call_target="tpu_custom_call" | custom-call | tf_op jit(solution)/shard_map/pallas_call | solution.py:716

commit v6 on v5

--- a/solution.py
+++ b/solution.py
@@ -433,14 +433,6 @@
     h_ra.start()
     h_la.start()
 
-    @pl.when(jnp.logical_not(fill_right))
-    def _():
-        h_rc.start()
-
-    @pl.when(jnp.logical_not(fill_left))
-    def _():
-        h_lc.start()
-
     landed(rb_d, br.at[2])
 
     zero = jnp.zeros((16, 128), F32)
@@ -522,6 +514,15 @@
     pk_row[...] = row_peak
     for p in x_others:
         tell_column(p).start()
+
+    @pl.when(jnp.logical_not(fill_right))
+    def _():
+        h_rc.start()
+
+    @pl.when(jnp.logical_not(fill_left))
+    def _():
+        h_lc.start()
+
     h_rd.start()
     h_ld.start()
     landed(rz_in.at[pl.ds(0, experts - 1)], wr.at[0])

time: 88.3 us -> 89.1 us (level)
  Pallas kernels: 87.2 us -> 88.3 us
    pallas_call x1, Pallas kernels: 84.6 us -> 85.7 us  [shards(): pl.pallas_call(functools.partial(kernel, experts, cap, tok, top), out_sha...]
where the time goes in v6:
time: 89.1 us; the launch traced here: 89 us
  Pallas kernels  88.3 us (99%)
    pallas_call x1, Pallas kernels, shards(): pl.pallas_call(functools.partial(kernel, experts, cap, tok, top), out_sha...  85.7 us
    pallas_call x1, Pallas kernels, shards(): pl.pallas_call(finish, out_shape=tuple((jax.ShapeDtypeStruct(*shape) for...  2.63 us

profile of v6, /device:TPU:1, one launch (start us, length us, event | category | flops | bytes accessed | tf_op | source)
XLA Modules:
  0.0 89.0 jit_solution(14706079400767049360)
XLA Ops:
  0.6 85.7 %shard_map.93 = (f32[384,1408]{1,0:T(8,128)S(1)}, f32[384,1408]{1,0:T(8,128)S(1)}, f32[768,1408]{1,0:T(8,128)S(1)}, bf16[96,768]{1,0:T(8,128)(2,1)S(1)}, bf16[96...) custom-call(bf16[64,3072]{1,0:T(8,128)(2,1)} %og.1, s32[4,64]{1,0:T(4,128)} %bitcast.15, ...), custom_call_target="tpu_custom_call" | custom-call | flops 6643777536 | bytes 4325376 | tf_op jit(solution)/shard_map/pallas_call | solution.py:662
  86.3 2.6 %shard_map.94 = (bf16[384,1408]{1,0:T(8,128)(2,1)}, bf16[384,1408]{1,0:T(8,128)(2,1)}, bf16[768,1408]{1,0:T(8,128)(2,1)}, f32[4,64]{1,0:T(4,128)}) custom-call(f32[384,1408]{1,0:T(8,128)S(1)} %get-tuple-element.15.a_gate, f32[384,1408]{1,0:T(8,128)S(1)} %get-tuple-element.16.a_up, f32[768,1408]{1,0:T(8,128)S(1)} %get-tuple-element.17.wg_acc, ...), custom_call_target="tpu_custom_call" | custom-call | tf_op jit(solution)/shard_map/pallas_call | solution.py:717
